TPU v7x, 128 devices: a whole 4x4x4 slice. The times are simulated.
128 devices in a mesh: src: 4 (over z), tm: 2 (over core), tile: 16 (over x, y).
Axes of the slice: x: 4, y: 4, z: 4, core: 2. Of those that a mesh axis runs over, the one named last changes fastest.
Arguments:
- latents: bfloat16 [16, 4, 32, 768], P('src', 'tm', 'tile'), may hold values from -6 to 6
- decoder_group: int32 [16, 1], replicated, may hold values from 0 to 3; in each aligned block of 4 rows (0 to 3, 4 to 7, ...) at most 2 rows name the same one
- frames: int32 [16], replicated, may hold values from 1 to 4
- conv_in: bfloat16 [3, 3, 3, 16, 384], replicated, may hold values from -0.3125 to 0.3125
- norm_gain: float32 [384], replicated, may hold values from 0.1 to 1.9
- conv_mid: bfloat16 [3, 3, 3, 384, 384], replicated, may hold values from -0.0625 to 0.0625
- conv_up: bfloat16 [3, 3, 384, 192], replicated, may hold values from -0.109375 to 0.109375
Outputs:
- decoded: bfloat16 [32, 4, 64, 18432], P('src', 'tm', 'tile')
Inputs may be any that keep to these rules, and one draw needn't show every extreme that they name: `decoder_group`: among the 4 clips of one sender at most 2 name the same group.
All inputs are finite; a program needn't handle non-finite values.
Results may differ from a plain program's by a relative error of at most 0.009.
Values may be sent and summed in bfloat16 or wider, within the bound.
A program may use at most 128 MiB of HBM per device.

v0:
```python
import jax
import jax.numpy as jnp
from jax import lax
from jax.sharding import PartitionSpec as P

CAP = 2


def padded(x, sides, width):
    for axis, dim in sides:
        devices, length = (lax.axis_size(axis), x.shape[dim])
        up = [(i, (i + 1) % devices) for i in range(devices - 1)]
        down = [(j, i) for i, j in up]
        last = lax.slice_in_dim(x, length - width, length, axis=dim)
        leading = lax.slice_in_dim(x, 0, width, axis=dim)
        before = lax.ppermute(last, axis, up)
        after = lax.ppermute(leading, axis, down)
        x = jnp.concatenate([before, x, after], axis=dim)
    return x


def from_behind(x, axis, by):
    devices = lax.axis_size(axis)
    pairs = [(i, i + by) for i in range(devices) if 0 <= i + by < devices]
    return lax.ppermute(x, axis, pairs)


def conv_time(extended, kernel):
    widened = jnp.pad(extended, ((0, 0), (0, 0), (0, 0), (1, 1), (0, 0)))
    return lax.conv_general_dilated(
        widened,
        kernel,
        (1, 1, 1),
        "VALID",
        dimension_numbers=("NDHWC", "DHWIO", "NDHWC"),
        preferred_element_type=jnp.float32,
    )


def activate(hidden_f, norm_gain):
    scaled = (
        hidden_f
        * lax.rsqrt(jnp.mean(hidden_f * hidden_f, axis=-1, keepdims=True) + 1e-06)
        * norm_gain
    )
    return jax.nn.silu(scaled).astype(jnp.bfloat16)


def decode(latent_slab, earlier_latent, earlier_active, conv_in, norm_gain, conv_mid, conv_up):
    slots, count_frames, rows, packed = latent_slab.shape
    in_channels = conv_in.shape[3]
    channels = conv_mid.shape[4]
    out_channels = conv_up.shape[3]
    width = packed // in_channels
    inputs = latent_slab.reshape(slots, count_frames, rows, width, in_channels)
    before = earlier_latent(inputs)
    extended = jnp.concatenate([before, inputs], axis=1)
    extended = padded(extended, (("tile", 2),), 1)
    hidden = conv_time(extended, conv_in).astype(jnp.bfloat16)
    hidden_f = hidden.astype(jnp.float32)
    active = activate(hidden_f, norm_gain)
    before_active = earlier_active(active[:, count_frames - 2 :])
    extended_active = jnp.concatenate([before_active, active], axis=1)
    extended_active = padded(extended_active, (("tile", 2),), 1)
    branch = conv_time(extended_active, conv_mid)
    residual = (hidden_f + branch).astype(jnp.bfloat16)
    doubled = jnp.repeat(jnp.repeat(residual, 2, axis=2), 2, axis=3)
    doubled = padded(doubled, (("tile", 2),), 1)
    flattened = doubled.reshape(slots * count_frames, 2 * rows + 2, 2 * width, channels)
    flattened = jnp.pad(flattened, ((0, 0), (0, 0), (1, 1), (0, 0)))
    upper = lax.conv_general_dilated(
        flattened,
        conv_up,
        (1, 1),
        "VALID",
        dimension_numbers=("NHWC", "HWIO", "NHWC"),
        preferred_element_type=jnp.float32,
    )
    return upper.reshape(slots, count_frames, 2 * rows, 2 * width * out_channels)


def per_device(latents, decoder_group, frames, conv_in, norm_gain, conv_mid, conv_up):
    groups = lax.axis_size("src")
    clips = latents.shape[0]
    slab = latents.shape[1]
    total_slots = groups * CAP
    targets = decoder_group[:, 0].reshape(groups, clips)
    same = targets[:, :, None] == targets[:, None, :]
    earlier = jnp.arange(clips)[None, :] < jnp.arange(clips)[:, None]
    ranks = jnp.sum(jnp.where(same & earlier[None], 1, 0), axis=2).astype(jnp.int32)
    slot_of = targets * CAP + ranks
    sender = lax.axis_index("src")
    my_slots = lax.dynamic_index_in_dim(slot_of, sender, 0, keepdims=False)
    selector = (jnp.arange(total_slots, dtype=jnp.int32)[:, None] == my_slots[None, :]).astype(
        jnp.bfloat16
    )
    outgoing = jnp.einsum(
        "ki,ifhc->kfhc", selector, latents, preferred_element_type=jnp.float32
    ).astype(jnp.bfloat16)
    lengths = frames.reshape(groups, clips)
    taken = (targets == sender)[:, :, None] & (
        ranks[:, :, None] == jnp.arange(CAP, dtype=jnp.int32)[None, None, :]
    )
    counts_all = jnp.sum(jnp.where(taken, lengths[:, :, None], 0), axis=1).reshape(total_slots)
    routed = lax.all_to_all(outgoing, "src", split_axis=0, concat_axis=0, tiled=True)

    def earlier_latent(tail):
        return from_behind(tail, "tm", 1)

    def earlier_active(tail):
        return from_behind(tail, "tm", 1)

    result = decode(routed, earlier_latent, earlier_active, conv_in, norm_gain, conv_mid, conv_up)
    frame_index = lax.axis_index("tm") * slab + jnp.arange(slab, dtype=jnp.int32)
    live = (frame_index[None, :] < counts_all[:, None]).astype(jnp.float32)
    return (result * live[:, :, None, None]).astype(jnp.bfloat16)


def solution(mesh):
    placed = (P("src", "tm", "tile", None), P(), P(), P(), P(), P(), P())
    return jax.shard_map(
        per_device,
        mesh=mesh,
        in_specs=placed,
        out_specs=P("src", "tm", "tile", None),
        check_vma=False,
    )
```

profile of v0, /device:TPU:4, one launch (start us, length us, event | category | flops | bytes accessed | tf_op | source)
XLA Modules:
  0.0 181.1 jit_solution(8834855633914883855)
XLA Ops:
  0.0 0.0 copy-start
  0.0 0.5 broadcast.54
  0.5 1.3 reduce.3
  1.8 0.1 reshape_squeeze.3
  1.9 0.2 select_reduce_fusion
  2.2 1.0 convolution_convert_fusion.1
  3.2 10.6 %all_to_all.5 = bf16[8,2,2,768]{3,2,1,0:T(2,128)(2,1)S(1)} all-to-all(bf16[8,2,2,768]{3,2,1,0:T(2,128)(2,1)S(1)} %copy.45), channel_id=1, replica_groups=mesh['src'=4,'tm'=2,'tile'=16] {'src'}, dimensions={0} | all-to-all | bytes 98304 | tf_op jit(solution)/shard_map/all_to_all | solution.py:105
  13.9 0.3 reshape.83
  14.2 1.3 collective-permute-start
  15.5 0.2 copy.48
  15.7 1.1 collective-permute-done
  16.8 0.2 copy.47
  17.0 0.1 fusion.26
  17.1 3.5 %collective-permute-start.1 = (bf16[8,4,1,48,16]{3,4,2,1,0:T(8,128)(2,1)S(1)}, bf16[8,4,1,48,16]{3,4,2,1,0:T(8,128)(2,1)S(1)}, u32[]{:S(2)}, u32[]{:S(2)}) collective-permute-start(bf16[8,4,1,48,16]{3,4,2,1,0:T(8,128)(2,1)S(1)} %get-tuple-element.9), channel_id=1, source_target_pairs={{0,1},{1,2},{2,3},{3,4},{4,5},{5,6},{6,7},{7,8},{8,9},{9,10},{10,1... | collective-permute-start | bytes 147464 | tf_op jit(solution)/shard_map/ppermute | solution.py:16
  20.6 4.5 %collective-permute-start.2 = (bf16[8,4,1,48,16]{3,4,2,1,0:T(8,128)(2,1)S(1)}, bf16[8,4,1,48,16]{3,4,2,1,0:T(8,128)(2,1)S(1)}, u32[]{:S(2)}, u32[]{:S(2)}) collective-permute-start(bf16[8,4,1,48,16]{3,4,2,1,0:T(8,128)(2,1)S(1)} %get-tuple-element.10), channel_id=1, source_target_pairs={{1,0},{2,1},{3,2},{4,3},{5,4},{6,5},{7,6},{8,7},{9,8},{10,9},{11,1... | collective-permute-start | bytes 147464 | tf_op jit(solution)/shard_map/ppermute | solution.py:17
  25.1 1.8 collective-permute-done.1
  26.9 1.2 collective-permute-done.2
  28.0 0.1 pad_maximum_fusion.1
  28.2 1.0 copy.49
  29.2 0.0 copy-start.3
  29.2 3.9 %fusion.14 = (f32[8,2,2,48]{0,3,2,1:T(8,128)S(1)}, bf16[8,2,2,48,384]{4,0,3,2,1:T(8,128)(2,1)}) fusion(bf16[8,4,4,48,16]{4,0,3,2,1:T(8,128)(2,1)S(1)} %copy.49, bf16[3,3,3,16,384]{4,3,2,1,0:T(8,128)(2,1)} %param.10), kind=kOutput, calls=%fused_computation.18 | convolution fusion | flops 504887808 | bytes 1714176 | tf_op jit(solution)/shard_map/conv_general_dilated | solution.py:30
  33.0 0.1 copy.50
  33.1 0.1 copy.51
  33.2 0.0 copy-done.3
  33.2 2.0 %fusion.21 = bf16[8,2,2,48,384]{4,0,3,2,1:T(8,128)(2,1)S(1)} fusion(bf16[8,2,2,48,384]{4,0,3,2,1:T(8,128)(2,1)} %get-tuple-element.12, f32[384]{0:T(512)S(1)} %copy-done.3, f32[8,2,2,48]{0,3,2,1:T(8,128)S(1)} %copy.51), kind=kLoop, calls=%fused_computation.25 | loop fusion | flops 4718592 | bytes 2366976 | tf_op jit(solution)/shard_map/convert_element_type | solution.py:46
  35.3 0.0 copy-start.2
  35.3 1.5 collective-permute-start.3
  36.8 2.4 %collective-permute-done.3 = bf16[8,2,2,48,384]{4,0,3,2,1:T(8,128)(2,1)S(1)} collective-permute-done((bf16[8,2,2,48,384]{4,0,3,2,1:T(8,128)(2,1)S(1)}, bf16[8,2,2,48,384]{4,0,3,2,1:T(8,128)(2,1)S(1)}, u32[]{:S(2)}, u32[]{:S(2)}) %collective-permute-start.3) | collective-permute-done | bytes 1179680 | tf_op jit(solution)/shard_map/ppermute | solution.py:25
  39.1 0.3 fusion.25
  39.4 3.4 %collective-permute-start.4 = (bf16[8,4,1,48,384]{4,0,3,2,1:T(8,128)(2,1)S(1)}, bf16[8,4,1,48,384]{4,0,3,2,1:T(8,128)(2,1)S(1)}, u32[]{:S(2)}, u32[]{:S(2)}) collective-permute-start(bf16[8,4,1,48,384]{4,0,3,2,1:T(8,128)(2,1)S(1)} %get-tuple-element.7), channel_id=1, source_target_pairs={{0,1},{1,2},{2,3},{3,4},{4,5},{5,6},{6,7},{7,8},{8,9},{9,10},{10,1... | collective-permute-start | bytes 3538952 | tf_op jit(solution)/shard_map/ppermute | solution.py:16
  42.8 5.2 %collective-permute-start.5 = (bf16[8,4,1,48,384]{4,0,3,2,1:T(8,128)(2,1)S(1)}, bf16[8,4,1,48,384]{4,0,3,2,1:T(8,128)(2,1)S(1)}, u32[]{:S(2)}, u32[]{:S(2)}) collective-permute-start(bf16[8,4,1,48,384]{4,0,3,2,1:T(8,128)(2,1)S(1)} %get-tuple-element.8), channel_id=1, source_target_pairs={{1,0},{2,1},{3,2},{4,3},{5,4},{6,5},{7,6},{8,7},{9,8},{10,9},{11,1... | collective-permute-start | bytes 3538952 | tf_op jit(solution)/shard_map/ppermute | solution.py:17
  48.0 24.4 %collective-permute-done.4 = bf16[8,4,1,48,384]{4,0,3,2,1:T(8,128)(2,1)S(1)} collective-permute-done((bf16[8,4,1,48,384]{4,0,3,2,1:T(8,128)(2,1)S(1)}, bf16[8,4,1,48,384]{4,0,3,2,1:T(8,128)(2,1)S(1)}, u32[]{:S(2)}, u32[]{:S(2)}) %collective-permute-start.4) | collective-permute-done | bytes 1179680 | tf_op jit(solution)/shard_map/ppermute | solution.py:16
  72.4 1.2 collective-permute-done.5
  73.6 0.0 copy-done.2
  73.6 27.4 %fusion.22 = bf16[8,2,2,48,384]{4,0,3,2,1:T(8,128)(2,1)S(1)} fusion(bf16[8,2,2,48,384]{4,0,3,2,1:T(8,128)(2,1)S(1)} %copy-done.2, bf16[3,3,3,384,384]{4,3,2,1,0:T(8,128)(2,1)} %param.12, bf16[8,4,1,48,384]{4,0,3,2,1:T(8,128)(2,1)S(1)} %collective-permute-done.5, bf16[8,2,2,48,384]{4,0,3,2,1:T(8,128)(2,1)S(1)} %fusion.21, ...), kind=kOutput, calls=%fused_computation.26 | convolution fusion | flops 12081364992 | bytes 15040512 | tf_op jit(solution)/shard_map/conv_general_dilated | solution.py:30
  101.0 1.6 copy.52
  102.7 1.2 broadcast_in_dim.42
  103.9 2.8 %broadcast_in_dim.43 = bf16[8,2,4,48,2,384]{5,1,0,4,3,2:T(2,128)(2,1)S(1)} broadcast(bf16[8,2,4,48,384]{4,1,0,3,2:T(2,128)(2,1)S(1)} %bitcast.27), dimensions={0,1,2,3,5} | broadcast | bytes 7077888 | tf_op jit(solution)/shard_map/broadcast_in_dim | solution.py:67
  106.7 0.0 copy-start.1
  106.7 0.0 copy-start.4
  106.8 3.0 %fusion.34 = (bf16[8,2,1,96,384]{4,1,0,3,2:T(2,128)(2,1)}, bf16[8,2,1,96,384]{4,1,0,3,2:T(2,128)(2,1)}) fusion(bf16[8,2,4,96,384]{4,1,0,3,2:T(2,128)(2,1)S(1)} %bitcast.26), kind=kLoop, calls=%fused_computation.55 | loop fusion | bytes 4718592 | tf_op jit(solution)/shard_map/slice | solution.py:14
  109.8 0.0 copy-done.1
  109.8 3.5 %collective-permute-start.6 = (bf16[8,2,1,96,384]{4,1,0,3,2:T(2,128)(2,1)}, bf16[8,2,1,96,384]{4,1,0,3,2:T(2,128)(2,1)}, u32[]{:S(2)}, u32[]{:S(2)}) collective-permute-start(bf16[8,2,1,96,384]{4,1,0,3,2:T(2,128)(2,1)} %get-tuple-element.5), channel_id=1, source_target_pairs={{0,1},{1,2},{2,3},{3,4},{4,5},{5,6},{6,7},{7,8},{8,9},{9,10},{10,1... | collective-permute-start | bytes 3538952 | tf_op jit(solution)/shard_map/ppermute | solution.py:16
  113.3 4.9 %collective-permute-start.7 = (bf16[8,2,1,96,384]{4,1,0,3,2:T(2,128)(2,1)}, bf16[8,2,1,96,384]{4,1,0,3,2:T(2,128)(2,1)S(1)}, u32[]{:S(2)}, u32[]{:S(2)}) collective-permute-start(bf16[8,2,1,96,384]{4,1,0,3,2:T(2,128)(2,1)} %get-tuple-element.6), channel_id=1, source_target_pairs={{1,0},{2,1},{3,2},{4,3},{5,4},{6,5},{7,6},{8,7},{9,8},{10,9},{11,1... | collective-permute-start | bytes 3538952 | tf_op jit(solution)/shard_map/ppermute | solution.py:17
  118.2 0.0 copy-done.4
  118.2 0.1 broadcast_in_dim.44
  118.3 0.1 select_reduce_fusion.1
  118.4 0.1 copy.54
  118.5 0.1 lt.45
  118.6 0.1 compare_convert_fusion
  118.7 10.8 %concatenate.27 = bf16[16,4,96,384]{3,0,2,1:T(8,128)(2,1)} reshape(bf16[8,2,4,48,2,384]{5,1,0,4,3,2:T(2,128)(2,1)} %copy-done.1) | data formatting | bytes 9437184 | tf_op jit(solution)/shard_map/concatenate | solution.py:18
  129.5 12.8 %collective-permute-done.6 = bf16[8,2,1,96,384]{4,1,0,3,2:T(2,128)(2,1)} collective-permute-done((bf16[8,2,1,96,384]{4,1,0,3,2:T(2,128)(2,1)}, bf16[8,2,1,96,384]{4,1,0,3,2:T(2,128)(2,1)}, u32[]{:S(2)}, u32[]{:S(2)}) %collective-permute-start.6) | collective-permute-done | bytes 1179680 | tf_op jit(solution)/shard_map/ppermute | solution.py:16
  142.3 3.7 %concatenate.26 = bf16[16,1,96,384]{3,0,2,1:T(8,128)(2,1)} reshape(bf16[8,2,1,96,384]{4,1,0,3,2:T(2,128)(2,1)} %collective-permute-done.6) | data formatting | bytes 2359296 | tf_op jit(solution)/shard_map/concatenate | solution.py:18
  146.0 0.0 collective-permute-done.7
  146.0 1.3 concatenate.28
  147.3 0.0 copy-done
  147.3 15.2 %fusion = f32[16,4,96,192]{3,0,2,1:T(8,128)S(1)} fusion(bf16[3,3,384,192]{2,3,1,0:T(8,128)(2,1)S(1)} %copy-done, bf16[16,1,96,384]{3,0,2,1:T(8,128)(2,1)} %concatenate.28, bf16[16,4,96,384]{3,0,2,1:T(8,128)(2,1)} %concatenate.27, bf16[16,1,96,384]{3,0,2,1:T(8,128)(2,1)} %concatenate.26), kind=kOutput, calls=%fused_computation | convolution fusion | flops 8118337536 | bytes 13123584 | tf_op jit(solution)/shard_map/conv_general_dilated | solution.py:71
  162.5 6.3 %copy.53 = f32[16,4,96,192]{3,2,1,0:T(8,128)} copy(f32[16,4,96,192]{3,0,2,1:T(8,128)S(1)} %fusion) | data formatting | bytes 9437184 | tf_op jit(solution)/shard_map/conv_general_dilated | solution.py:71
  168.8 7.6 %reshape.86 = f32[8,2,4,18432]{3,2,1,0:T(4,128)} reshape(f32[16,4,96,192]{3,2,1,0:T(8,128)} %copy.53) | data formatting | bytes 9437184 | tf_op jit(solution)/shard_map/reshape | solution.py:79
  176.4 4.8 %multiply_convert_fusion = bf16[8,2,4,18432]{3,2,1,0:T(4,128)(2,1)} fusion(f32[8,2,4,18432]{3,2,1,0:T(4,128)} %reshape.86, f32[8,2]{1,0:T(8,128)S(1)} %compare_convert_fusion), kind=kLoop, calls=%fused_computation.14 | loop fusion | flops 2359296 | bytes 7077952 | tf_op jit(solution)/shard_map/convert_element_type | solution.py:116
  (8 shorter events, 0.1 us)
Async XLA Ops:
  0.0 147.3 %copy-start = (bf16[3,3,384,192]{2,3,1,0:T(8,128)(2,1)S(1)}, bf16[3,3,384,192]{2,3,1,0:T(8,128)(2,1)}, u32[]{:S(2)}) copy-start(bf16[3,3,384,192]{2,3,1,0:T(8,128)(2,1)} %param.13) | copy-start | bytes 3981316
  14.2 2.6 %collective-permute-start = (bf16[8,2,2,48,16]{4,3,0,2,1:T(8,128)(2,1)S(1)}, bf16[8,2,2,48,16]{4,3,0,2,1:T(8,128)(2,1)S(1)}, u32[]{:S(2)}, u32[]{:S(2)}) collective-permute-start(bf16[8,2,2,48,16]{4,3,0,2,1:T(8,128)(2,1)S(1)} %reshape.83), channel_id=1, source_target_pairs={{0,16},{1,17},{2,18},{3,19},{4,20},{5,21},{6,22},{7,23},{8,24},{9,... | collective-permute-start | bytes 147464 | tf_op jit(solution)/shard_map/ppermute | solution.py:25
  17.1 9.8 %collective-permute-start.1 = (bf16[8,4,1,48,16]{3,4,2,1,0:T(8,128)(2,1)S(1)}, bf16[8,4,1,48,16]{3,4,2,1,0:T(8,128)(2,1)S(1)}, u32[]{:S(2)}, u32[]{:S(2)}) collective-permute-start(bf16[8,4,1,48,16]{3,4,2,1,0:T(8,128)(2,1)S(1)} %get-tuple-element.9), channel_id=1, source_target_pairs={{0,1},{1,2},{2,3},{3,4},{4,5},{5,6},{6,7},{7,8},{8,9},{9,10},{10,1... | collective-permute-start | bytes 147464 | tf_op jit(solution)/shard_map/ppermute | solution.py:16
  20.6 7.5 %collective-permute-start.2 = (bf16[8,4,1,48,16]{3,4,2,1,0:T(8,128)(2,1)S(1)}, bf16[8,4,1,48,16]{3,4,2,1,0:T(8,128)(2,1)S(1)}, u32[]{:S(2)}, u32[]{:S(2)}) collective-permute-start(bf16[8,4,1,48,16]{3,4,2,1,0:T(8,128)(2,1)S(1)} %get-tuple-element.10), channel_id=1, source_target_pairs={{1,0},{2,1},{3,2},{4,3},{5,4},{6,5},{7,6},{8,7},{9,8},{10,9},{11,1... | collective-permute-start | bytes 147464 | tf_op jit(solution)/shard_map/ppermute | solution.py:17
  29.2 4.1 %copy-start.3 = (f32[384]{0:T(512)S(1)}, f32[384]{0:T(512)}, u32[]{:S(2)}) copy-start(f32[384]{0:T(512)} %param.11) | copy-start | bytes 4612
  35.3 38.3 %copy-start.2 = (bf16[8,2,2,48,384]{4,0,3,2,1:T(8,128)(2,1)S(1)}, bf16[8,2,2,48,384]{4,0,3,2,1:T(8,128)(2,1)}, u32[]{:S(2)}) copy-start(bf16[8,2,2,48,384]{4,0,3,2,1:T(8,128)(2,1)} %get-tuple-element.12) | copy-start | bytes 3538948
  35.3 3.9 %collective-permute-start.3 = (bf16[8,2,2,48,384]{4,0,3,2,1:T(8,128)(2,1)S(1)}, bf16[8,2,2,48,384]{4,0,3,2,1:T(8,128)(2,1)S(1)}, u32[]{:S(2)}, u32[]{:S(2)}) collective-permute-start(bf16[8,2,2,48,384]{4,0,3,2,1:T(8,128)(2,1)S(1)} %fusion.21), channel_id=1, source_target_pairs={{0,16},{1,17},{2,18},{3,19},{4,20},{5,21},{6,22},{7,23},{8,24},{9,... | collective-permute-start | bytes 3538952 | tf_op jit(solution)/shard_map/ppermute | solution.py:25
  39.4 33.0 %collective-permute-start.4 = (bf16[8,4,1,48,384]{4,0,3,2,1:T(8,128)(2,1)S(1)}, bf16[8,4,1,48,384]{4,0,3,2,1:T(8,128)(2,1)S(1)}, u32[]{:S(2)}, u32[]{:S(2)}) collective-permute-start(bf16[8,4,1,48,384]{4,0,3,2,1:T(8,128)(2,1)S(1)} %get-tuple-element.7), channel_id=1, source_target_pairs={{0,1},{1,2},{2,3},{3,4},{4,5},{5,6},{6,7},{7,8},{8,9},{9,10},{10,1... | collective-permute-start | bytes 3538952 | tf_op jit(solution)/shard_map/ppermute | solution.py:16
  42.8 30.7 %collective-permute-start.5 = (bf16[8,4,1,48,384]{4,0,3,2,1:T(8,128)(2,1)S(1)}, bf16[8,4,1,48,384]{4,0,3,2,1:T(8,128)(2,1)S(1)}, u32[]{:S(2)}, u32[]{:S(2)}) collective-permute-start(bf16[8,4,1,48,384]{4,0,3,2,1:T(8,128)(2,1)S(1)} %get-tuple-element.8), channel_id=1, source_target_pairs={{1,0},{2,1},{3,2},{4,3},{5,4},{6,5},{7,6},{8,7},{9,8},{10,9},{11,1... | collective-permute-start | bytes 3538952 | tf_op jit(solution)/shard_map/ppermute | solution.py:17
  106.7 3.0 %copy-start.1 = (bf16[8,2,4,48,2,384]{5,1,0,4,3,2:T(2,128)(2,1)}, bf16[8,2,4,48,2,384]{5,1,0,4,3,2:T(2,128)(2,1)S(1)}, u32[]{:S(2)}) copy-start(bf16[8,2,4,48,2,384]{5,1,0,4,3,2:T(2,128)(2,1)S(1)} %broadcast_in_dim.43) | copy-start | bytes 14155780
  106.7 11.5 %copy-start.4 = (s32[16]{0:T(128)S(1)}, s32[16]{0:T(128)}, u32[]{:S(2)}) copy-start(s32[16]{0:T(128)} %param.9) | copy-start | bytes 196
  109.8 32.5 %collective-permute-start.6 = (bf16[8,2,1,96,384]{4,1,0,3,2:T(2,128)(2,1)}, bf16[8,2,1,96,384]{4,1,0,3,2:T(2,128)(2,1)}, u32[]{:S(2)}, u32[]{:S(2)}) collective-permute-start(bf16[8,2,1,96,384]{4,1,0,3,2:T(2,128)(2,1)} %get-tuple-element.5), channel_id=1, source_target_pairs={{0,1},{1,2},{2,3},{3,4},{4,5},{5,6},{6,7},{7,8},{8,9},{9,10},{10,1... | collective-permute-start | bytes 3538952 | tf_op jit(solution)/shard_map/ppermute | solution.py:16
  113.3 32.7 %collective-permute-start.7 = (bf16[8,2,1,96,384]{4,1,0,3,2:T(2,128)(2,1)}, bf16[8,2,1,96,384]{4,1,0,3,2:T(2,128)(2,1)S(1)}, u32[]{:S(2)}, u32[]{:S(2)}) collective-permute-start(bf16[8,2,1,96,384]{4,1,0,3,2:T(2,128)(2,1)} %get-tuple-element.6), channel_id=1, source_target_pairs={{1,0},{2,1},{3,2},{4,3},{5,4},{6,5},{7,6},{8,7},{9,8},{10,9},{11,1... | collective-permute-start | bytes 3538952 | tf_op jit(solution)/shard_map/ppermute | solution.py:17
where the time goes:
time: 182 us; the launch traced here: 181 us
  matrix products  47.5 us (26%)
  waiting for transfers between devices  44.8 us (25%)
  local copies, waits for them, and re-layouts  41.1 us (23%)
  starting transfers between devices  27.8 us (15%)
  blocking collectives  10.6 us (6%)
  other arithmetic  9.01 us (5%)
    ppermute x3, waiting for transfers between devices, padded(): before = lax.ppermute(last, axis, up)  38.9 us
    conv_general_dilated x2, matrix products, conv_time(): lax.conv_general_dilated(widened, kernel, (1, 1, 1), 'VALID', dimension_n...  31.3 us
    concatenate x4, local copies, waits for them, and re-layouts, padded(): x = jnp.concatenate([before, x, after], axis=dim)  16.8 us
    conv_general_dilated x1, matrix products, decode(): lax.conv_general_dilated(flattened, conv_up, (1, 1), 'VALID', dimension_n...  15.2 us
    ppermute x3, starting transfers between devices, padded(): after = lax.ppermute(leading, axis, down)  14.5 us
    all_to_all x1, blocking collectives, per_device(): lax.all_to_all(outgoing, 'src', split_axis=0, concat_axis=0, tiled=True)  10.6 us
    ppermute x3, starting transfers between devices, padded(): before = lax.ppermute(last, axis, up)  10.4 us
    reshape x1, local copies, waits for them, and re-layouts, decode(): upper.reshape(slots, count_frames, 2 * rows, 2 * width * out_channels)  7.6 us
  transfers between devices with their start and end apart: 8, of which 7 were waited for; matrix products, arithmetic and copies ran while one was open for 8% of the time, Pallas kernels for 0%

commit v1 on v0

v1 whole, which is shorter than its diff:
```python
import functools

import jax
import jax.numpy as jnp
from jax import lax
from jax.experimental import pallas as pl
from jax.experimental.pallas import tpu as pltpu
from jax.sharding import PartitionSpec as P

CAP = 2
FR = 4
REACH = 2
MESH = pl.DeviceIdType.MESH
BF = jnp.bfloat16
F32 = jnp.float32


def shift_down(x, first):
    return jnp.where(first, 0.0, pltpu.roll(x, 1, x.ndim - 2))


def shift_up(x, last):
    return jnp.where(last, 0.0, pltpu.roll(x, x.shape[-2] - 1, x.ndim - 2))


def exchange_kernel(
    groups, tiles, group_ref, lat_ref, cin_ref, cup_ref, recv_ref, band_ref, up_ref, out_ref, send_sem, recv_sem, fwd_send, fwd_recv
):
    src, tm, tile = lax.axis_index("src"), lax.axis_index("tm"), lax.axis_index("tile")
    clips = 4
    taps = 2 * REACH + 1

    def ok(d):
        return jnp.logical_and(tile + d >= 0, tile + d < tiles)

    partners = [(k, d) for d in (0, 1, -1, 2, -2) for k in range(groups) if (k, d) != (0, 0)]

    barrier = pltpu.get_barrier_semaphore()
    for k, d in partners:
        @pl.when(ok(d))
        def _(k=k, d=d):
            pl.semaphore_signal(
                barrier, inc=1, device_id={"src": lax.rem(src + k, groups), "tile": tile + d}, device_id_type=MESH
            )
    pl.semaphore_signal(barrier, inc=1, device_id={"tm": 1 - tm}, device_id_type=MESH)

    for g in range(groups):
        parts = []
        for k in range(CAP):
            rank_of = []
            total = jnp.zeros((lat_ref.shape[0], 128), F32)
            for i in range(clips):
                target = group_ref[src * clips + i, 0]
                rank = jnp.int32(0)
                for e in range(i):
                    rank = rank + jnp.where(group_ref[src * clips + e, 0] == target, 1, 0)
                mine = jnp.where(jnp.logical_and(target == g, rank == k), 1.0, 0.0)
                block = lat_ref[:, 128 * (i // 2) : 128 * (i // 2) + 128].astype(F32)
                if i % 2 != k:
                    block = pltpu.roll(block, 64, 1)
                total = total + block * mine
            parts.append(total)
        lane = lax.broadcasted_iota(jnp.int32, parts[0].shape, 1)
        out_ref[g] = jnp.where(lane < 64, parts[0], parts[1]).astype(BF)

    nd = jnp.int32(1)
    for d in (-2, -1, 1, 2):
        nd = nd + jnp.where(ok(d), 1, 0)
    pl.semaphore_wait(barrier, groups * nd)

    def copy(k, d):
        g = lax.rem(src + k, groups)
        return pltpu.make_async_remote_copy(
            src_ref=out_ref.at[g],
            dst_ref=recv_ref.at[tm, REACH - d, src],
            send_sem=send_sem.at[d + REACH, k],
            recv_sem=recv_sem.at[REACH - d, src],
            device_id={"src": g, "tile": tile + d},
            device_id_type=MESH,
        )

    for k, d in partners:
        @pl.when(ok(d))
        def _(k=k, d=d):
            copy(k, d).start()

    recv_ref[tm, REACH, src] = out_ref[src]

    for d in (-2, -1, 1, 2):
        @pl.when(jnp.logical_not(ok(d)))
        def _(d=d):
            recv_ref[tm, d + REACH] = jnp.zeros(recv_ref.shape[2:], BF)

    @pl.when(tm == 0)
    def _():
        recv_ref[1] = jnp.zeros(recv_ref.shape[1:], BF)

    zero = jnp.zeros((16, cin_ref.shape[-1]), BF)
    n = cin_ref.shape[-1]
    for f in range(FR):
        for c in range(3):
            for row in range(4):
                for t in range(FR):
                    for q in range(2):
                        a, b = t - f + 2, row - q
                        inside = 0 <= a <= 2 and 0 <= b <= 2
                        value = cin_ref[a, b, c] if inside else zero
                        at = ((c * 4 + row) * FR + t) * 16
                        band_ref[f, at : at + 16, q * n : (q + 1) * n] = value

    depth, width = cup_ref.shape[-2:]
    step = 96
    def fold(s, _):
        at = pl.multiple_of(s * step, step)
        for p in range(2):
            for i in range(2):
                rows = ((0,), (1, 2)) if p == 0 else ((0, 1), (2,))
                per_c = []
                for c in range(3):
                    terms = [cup_ref[b, c, pl.ds(at, step), :].astype(F32) for b in rows[i]]
                    per_c.append(functools.reduce(jnp.add, terms))
                k0, k1, k2 = per_c
                up_ref[p, pl.ds(i * depth + at, step), :] = jnp.concatenate(
                    [k1 + k2, k0 + k1, k0, k2], axis=-1
                ).astype(BF)
        return 0

    lax.fori_loop(0, depth // step, fold, 0)

    def forward(d):
        return pltpu.make_async_remote_copy(
            src_ref=recv_ref.at[0, d + REACH],
            dst_ref=recv_ref.at[0, d + REACH],
            send_sem=fwd_send.at[d + REACH],
            recv_sem=fwd_recv.at[d + REACH],
            device_id={"tm": 1 - tm},
            device_id_type=MESH,
        )

    for d in (0, 1, -1, 2, -2):
        for k in range(groups):
            if (k, d) == (0, 0):
                continue
            s = lax.rem(src + k, groups)

            @pl.when(ok(d))
            def _(d=d, s=s):
                pltpu.make_async_remote_copy(
                    src_ref=out_ref.at[0],
                    dst_ref=recv_ref.at[tm, d + REACH, s],
                    send_sem=send_sem.at[d + REACH, 0],
                    recv_sem=recv_sem.at[d + REACH, s],
                    device_id={"tm": 1 - tm},
                    device_id_type=MESH,
                ).wait_recv()

        @pl.when(tm == 0)
        def _(d=d):
            forward(d).start()

    for k, d in partners:
        @pl.when(ok(d))
        def _(k=k, d=d):
            copy(k, d).wait_send()

    for d in (0, 1, -1, 2, -2):
        @pl.when(tm == 0)
        def _(d=d):
            forward(d).wait_send()

        @pl.when(tm == 1)
        def _(d=d):
            forward(d).wait_recv()


def decode_kernel(
    groups,
    tiles,
    group_ref,
    frames_ref,
    recv_ref,
    gain_ref,
    band_hbm,
    mid_hbm,
    up_hbm,
    out_hbm,
    count_ref,
    band_ref,
    mid_ref,
    up_ref,
    z_ref,
    act_ref,
    hid_ref,
    acc_ref,
    res_ref,
    y_ref,
    o_ref,
    zero_ref,
    used_ref,
    band_sem,
    mid_sem,
    up_sem,
    zero_sem,
    o_sem,
):
    src, tm, tile = lax.axis_index("src"), lax.axis_index("tm"), lax.axis_index("tile")
    clips, slots = 4, groups * CAP
    C = gain_ref.shape[-1]
    Wd = z_ref.shape[1]
    top, bottom = tile == 0, tile == tiles - 1

    bands = [pltpu.make_async_copy(band_hbm.at[f], band_ref.at[f], band_sem.at[f]) for f in range(FR)]
    for band in bands:
        band.start()
    mids = []
    for a in (2, 1, 0):
        for b in range(3):
            for c in range(3):
                mids.append(
                    pltpu.make_async_copy(
                        mid_hbm.at[a, b, c],
                        mid_ref.at[a, pl.ds(b * C, C), pl.ds(c * C, C)],
                        mid_sem.at[a, b, c],
                    )
                )
    for mid in mids:
        mid.start()
    ups = pltpu.make_async_copy(up_hbm, up_ref, up_sem)
    ups.start()

    for s in range(slots):
        count_ref[s] = 0
    for s in range(groups):
        seen = jnp.int32(0)
        for i in range(clips):
            hit = group_ref[s * clips + i, 0] == src

            @pl.when(hit)
            def _(s=s, i=i, seen=seen):
                count_ref[s * CAP + jnp.minimum(seen, CAP - 1)] = frames_ref[s * clips + i]

            seen = seen + jnp.where(hit, 1, 0)

    zero_ref[...] = jnp.zeros(zero_ref.shape, BF)

    def clear(s, o):
        return pltpu.make_async_copy(zero_ref, out_hbm.at[s, o], zero_sem.at[s, o])

    def each_dead(go):
        def body(s, _):
            for o in range(2):
                @pl.when(2 * tm + o >= count_ref[s])
                def _():
                    go(clear(s, o))
            return 0
        lax.fori_loop(0, slots, body, 0)

    each_dead(lambda c: c.start())
    used_ref[0] = 0
    for band in bands:
        band.wait()

    lane = lax.broadcasted_iota(jnp.int32, (Wd, 128), 1)
    spot = lax.broadcasted_iota(jnp.int32, (Wd, 1), 0)
    gain = gain_ref[...]

    def first(s, _):
        n = count_ref[s]
        need = jnp.where(tm == 0, jnp.minimum(n, 2), jnp.where(n >= 3, n, 0))

        @pl.when(need > 0)
        def _():
            sender, k = s // CAP, lax.rem(s, CAP)
            for m in range(4):
                upper = [recv_ref[h, m, sender].astype(F32) for h in range(2)]
                lower = [recv_ref[h, m + 1, sender].astype(F32) for h in range(2)]
                z0 = pltpu.roll(upper[0], 96 - 64 * k, 1)
                z1 = pltpu.roll(upper[1], lax.rem(128 - 64 * k, 128), 1)
                z2 = pltpu.roll(lower[0], 64 - 64 * k, 1)
                z3 = pltpu.roll(lower[1], 96 - 64 * k, 1)
                z = jnp.where(lane < 32, z0, jnp.where(lane < 64, z1, jnp.where(lane < 96, z2, z3)))
                at = slice(128 * m, 128 * m + 128)
                z_ref[0, :, at] = shift_down(z, spot == 0).astype(BF)
                z_ref[1, :, at] = z.astype(BF)
                z_ref[2, :, at] = shift_up(z, spot == Wd - 1).astype(BF)

            for f in range(FR):
                @pl.when(f < need)
                def _(f=f):
                    lhs = jnp.concatenate(
                        [
                            jnp.concatenate([z_ref[c, :, 128 * j : 128 * j + 256] for c in range(3)], axis=1)
                            for j in range(3)
                        ],
                        axis=0,
                    )
                    h = jnp.dot(lhs, band_ref[f], preferred_element_type=F32)
                    for q in range(2):
                        hb = h[:, q * C : (q + 1) * C].astype(BF)
                        hf = hb.astype(F32)
                        ms = jnp.sum(hf * hf, axis=-1, keepdims=True) * (1.0 / C)
                        x = hf * lax.rsqrt(ms + 1e-06) * gain
                        act = x / (1.0 + jnp.exp(-x))
                        for j in range(3):
                            part = act[j * Wd : (j + 1) * Wd]
                            if j == 0:
                                part = jnp.where(top, 0.0, part)
                            if j == 2:
                                part = jnp.where(bottom, 0.0, part)
                            r = 2 * j + q
                            act_ref[s, f, r] = part.astype(BF)
                            if 1 <= r <= 4:
                                hid_ref[s, f, r - 1] = hb[j * Wd : (j + 1) * Wd]
        return 0

    lax.fori_loop(0, slots, first, 0)
    for mid in mids:
        mid.wait()
    ups.wait()

    spot4 = lax.broadcasted_iota(jnp.int32, (4, Wd, 1), 1)
    spot2 = lax.broadcasted_iota(jnp.int32, (2, Wd, 1), 1)
    left = lax.broadcasted_iota(jnp.int32, (2, Wd, C), 2) < C // 2

    def second(u, _):
        s, o = u // 2, lax.rem(u, 2)
        f = 2 * tm + o

        @pl.when(f < count_ref[s])
        def _():
            acc_ref[...] = jnp.zeros(acc_ref.shape, F32)

            def tap(a, _):
                x = act_ref[s, f - 2 + a]
                lhs = jnp.concatenate([x[b : b + 4].reshape(4 * Wd, C) for b in range(3)], axis=1)
                acc_ref[...] += jnp.dot(lhs, mid_ref[a], preferred_element_type=F32)
                return 0

            lax.fori_loop(jnp.maximum(2 - f, 0), 3, tap, 0)
            total = acc_ref[:, C : 2 * C].reshape(4, Wd, C) + hid_ref[s, f].astype(F32)
            total = total + shift_down(acc_ref[:, :C].reshape(4, Wd, C), spot4 == 0)
            total = total + shift_up(acc_ref[:, 2 * C :].reshape(4, Wd, C), spot4 == Wd - 1)
            for r in range(4):
                part = total[r]
                if r == 0:
                    part = jnp.where(top, 0.0, part)
                if r == 3:
                    part = jnp.where(bottom, 0.0, part)
                res_ref[r] = part.astype(BF)

            for p in range(2):
                lhs = jnp.concatenate(
                    [res_ref[p : p + 2].reshape(2 * Wd, C), res_ref[p + 1 : p + 3].reshape(2 * Wd, C)], axis=1
                )
                y = jnp.dot(lhs, up_ref[p], preferred_element_type=F32)
                still = y[:, :C].reshape(2, Wd, C)
                moved = y[:, C:].reshape(2, Wd, C)
                y = still + jnp.where(left, shift_down(moved, spot2 == 0), shift_up(moved, spot2 == Wd - 1))
                for h in range(2):
                    for v in range(C // 128):
                        y_ref[v, pl.ds((2 * h + p) * Wd, Wd), :] = y[h, :, v * 128 : v * 128 + 128]

            used = used_ref[0]
            buf = lax.rem(used, 2)

            @pl.when(used >= 2)
            def _():
                pltpu.make_async_copy(o_ref.at[buf], out_hbm.at[s, o], o_sem.at[buf]).wait()

            for w in range(Wd):
                for v in range(C // 128):
                    at = w * C + v * 128
                    o_ref[buf, :, at : at + 128] = y_ref[v, pl.ds(w, 4, stride=Wd), :].astype(BF)
            pltpu.make_async_copy(o_ref.at[buf], out_hbm.at[s, o], o_sem.at[buf]).start()
            used_ref[0] = used + 1
        return 0

    lax.fori_loop(0, 2 * slots, second, 0)

    used = used_ref[0]
    for last in range(2):
        @pl.when(used > last)
        def _(last=last):
            buf = lax.rem(used - 1 - last, 2)
            pltpu.make_async_copy(o_ref.at[buf], out_hbm.at[0, 0], o_sem.at[buf]).wait()
    each_dead(lambda c: c.wait())


def per_device(latents, decoder_group, frames, conv_in, norm_gain, conv_mid, conv_up):
    groups, tiles = lax.axis_size("src"), lax.axis_size("tile")
    clips, slab, rows, packed = latents.shape
    lc, C = conv_in.shape[3:]
    width = packed // lc
    out_c = conv_up.shape[-1]
    slots = groups * CAP
    lat = latents.reshape(clips, slab, rows, width, lc).transpose(3, 0, 2, 1, 4).reshape(width, -1)
    vmem = pl.BlockSpec(memory_space=pltpu.VMEM)
    smem = pl.BlockSpec(memory_space=pltpu.SMEM)
    hbm = pl.BlockSpec(memory_space=pl.ANY)
    taps = 2 * REACH + 1
    recv, band, up = pl.pallas_call(
        functools.partial(exchange_kernel, groups, tiles),
        out_shape=(
            jax.ShapeDtypeStruct((2, taps, groups, width, 128), BF),
            jax.ShapeDtypeStruct((FR, 3 * 4 * FR * lc, 2 * C), BF),
            jax.ShapeDtypeStruct((2, 2 * C, 4 * out_c), BF),
        ),
        in_specs=[smem, vmem, vmem, vmem],
        out_specs=(vmem, vmem, vmem),
        scratch_shapes=[
            pltpu.VMEM((groups, width, 128), BF),
            pltpu.SemaphoreType.DMA((taps, groups)),
            pltpu.SemaphoreType.DMA((taps, groups)),
            pltpu.SemaphoreType.DMA((taps,)),
            pltpu.SemaphoreType.DMA((taps,)),
        ],
        compiler_params=pltpu.CompilerParams(
            collective_id=0, has_side_effects=True, vmem_limit_bytes=32 * 1024 * 1024
        ),
    )(decoder_group, lat, conv_in, conv_up)

    return pl.pallas_call(
        functools.partial(decode_kernel, groups, tiles),
        out_shape=jax.ShapeDtypeStruct((slots, slab, 2 * rows, 2 * width * out_c), BF),
        in_specs=[smem, smem, vmem, vmem, hbm, hbm, hbm],
        out_specs=hbm,
        scratch_shapes=[
            pltpu.SMEM((slots,), jnp.int32),
            pltpu.VMEM(band.shape, BF),
            pltpu.VMEM((3, 3 * C, 3 * C), BF),
            pltpu.VMEM(up.shape, BF),
            pltpu.VMEM((3, width, 4 * FR * lc * 2), BF),
            pltpu.VMEM((slots, FR, 6, width, C), BF),
            pltpu.VMEM((slots, FR, 4, width, C), BF),
            pltpu.VMEM((4 * width, 3 * C), F32),
            pltpu.VMEM((4, width, C), BF),
            pltpu.VMEM((C // 128, 4 * width, 128), F32),
            pltpu.VMEM((2, 2 * rows, 2 * width * out_c), BF),
            pltpu.VMEM((2 * rows, 2 * width * out_c), BF),
            pltpu.SMEM((1,), jnp.int32),
            pltpu.SemaphoreType.DMA((FR,)),
            pltpu.SemaphoreType.DMA((3, 3, 3)),
            pltpu.SemaphoreType.DMA,
            pltpu.SemaphoreType.DMA((slots, 2)),
            pltpu.SemaphoreType.DMA((2,)),
        ],
        compiler_params=pltpu.CompilerParams(vmem_limit_bytes=56 * 1024 * 1024),
    )(decoder_group, frames, recv, norm_gain.reshape(1, C), band, conv_mid, up)


def solution(mesh):
    placed = (P("src", "tm", "tile", None), P(), P(), P(), P(), P(), P())
    return jax.shard_map(
        per_device,
        mesh=mesh,
        in_specs=placed,
        out_specs=P("src", "tm", "tile", None),
        check_vma=False,
    )
```

time: 182 us -> 53.8 us (0.30)
  the two profiles are of different devices: /device:TPU:4 before, /device:TPU:39 now
where the time goes in v1:
time: 53.8 us; the launch traced here: 53.5 us
  Pallas kernels  43.4 us (81%)
  local copies, waits for them, and re-layouts  10 us (19%)
    pallas_call x1, Pallas kernels, per_device(): pl.pallas_call(functools.partial(decode_kernel, groups, tiles), out_shape...  29.5 us
    pallas_call x1, Pallas kernels, per_device(): pl.pallas_call(functools.partial(exchange_kernel, groups, tiles), out_sha...  13.9 us
    unnamed x12, local copies, waits for them, and re-layouts  7.6 us
    reshape x1, local copies, waits for them, and re-layouts, per_device(): norm_gain.reshape(1, C)  1.3 us

profile of v1, /device:TPU:39, one launch (start us, length us, event | category | flops | bytes accessed | tf_op | source)
XLA Modules:
  0.0 53.5 jit_solution(2396107665513837293)
XLA Ops:
  0.0 0.0 copy-start.3
  0.0 1.3 %reshape.11.gain_ref = f32[1,384]{1,0:T(1,128)} reshape(f32[384]{0:T(512)} %param.11) | data formatting | bytes 3072 | tf_op jit(solution)/shard_map/reshape | solution.py:448
  1.3 0.7 %copy.16.group_ref = s32[16,1]{1,0:T(8,128)S(1)} copy(s32[16,1]{0,1:T(1,128)} %param.8) | data formatting | bytes 128 | tf_op args[1]
  2.0 0.0 copy-start.4
  2.0 0.9 %reshape.9 = bf16[4,2,2,48,16]{4,3,2,1,0:T(8,128)(2,1)S(1)} reshape(bf16[4,2,2,768]{3,2,1,0:T(2,128)(2,1)} %param.7) | data formatting | bytes 49152 | tf_op jit(solution)/shard_map/reshape | solution.py:396
  3.0 0.1 copy.12
  3.1 0.1 copy.14.lat_ref
  3.2 2.5 %copy.15.cup_ref = bf16[3,3,384,192]{3,2,1,0:T(8,128)(2,1)S(1)} copy(bf16[3,3,384,192]{2,3,1,0:T(8,128)(2,1)} %param.13) | data formatting | bytes 2654208 | tf_op args[6]
  5.7 0.0 copy-done.3
  5.7 13.9 %shard_map.73 = (bf16[2,5,4,48,128]{4,3,2,1,0:T(8,128)(2,1)S(1)}, bf16[4,768,768]{2,1,0:T(8,128)(2,1)S(1)}, bf16[2,768,768]{2,1,0:T(8,128)(2,1)S(1)}) custom-call(s32[16,1]{1,0:T(8,128)S(1)} %copy.16.group_ref, bf16[48,256]{1,0:T(8,128)(2,1)S(1)} %copy.14.lat_ref, bf16[3,3,3,16,384]{4,3,2,1,0:T(8,128)(2,1)S(1)} %copy-done.3, ...), custom_call_target="tpu_custom_call" | custom-call | tf_op jit(solution)/shard_map/pallas_call | solution.py:401
  19.7 0.0 copy-done.4
  19.7 0.0 copy-start
  19.7 2.1 %copy-done = bf16[4,768,768]{2,1,0:T(8,128)(2,1)} copy-done((bf16[4,768,768]{2,1,0:T(8,128)(2,1)}, bf16[4,768,768]{2,1,0:T(8,128)(2,1)S(1)}, u32[]{:S(2)}) %copy-start) | copy-done | bytes 4718616
  21.8 0.0 copy-start.1
  21.8 1.4 %copy-done.1 = bf16[2,768,768]{2,1,0:T(8,128)(2,1)} copy-done((bf16[2,768,768]{2,1,0:T(8,128)(2,1)}, bf16[2,768,768]{2,1,0:T(8,128)(2,1)S(1)}, u32[]{:S(2)}) %copy-start.1) | copy-done | bytes 2359320
  23.3 0.0 copy-start.2
  23.3 0.8 %copy-done.2 = bf16[2,5,4,48,128]{4,3,2,1,0:T(8,128)(2,1)} copy-done((bf16[2,5,4,48,128]{4,3,2,1,0:T(8,128)(2,1)}, bf16[2,5,4,48,128]{4,3,2,1,0:T(8,128)(2,1)S(1)}, u32[]{:S(2)}) %copy-start.2) | copy-done | bytes 491544
  24.0 29.5 %shard_map.74 = bf16[8,2,4,18432]{3,2,1,0:T(4,128)(2,1)} custom-call(s32[16,1]{1,0:T(8,128)} %copy-done.4, s32[16]{0:T(128)} %frames_ref.1, bf16[2,5,4,48,128]{4,3,2,1,0:T(8,128)(2,1)} %copy-done.2, f32[1,384]{1,0:T(1,128)} %reshape.11.gain_ref, bf16[4,768,768]{2,1,0:T(8,128)(2,1)} %copy-done, bf16[3,3,3,384,384]{4,3,2,1,0:T(8,128)(2,1)} %mid_hbm.1, ...), custom_call_target="tpu_custom_call" | custom-call | tf_op jit(solution)/shard_map/pallas_call | solution.py:422
Async XLA Ops:
  0.0 5.7 %copy-start.3 = (bf16[3,3,3,16,384]{4,3,2,1,0:T(8,128)(2,1)S(1)}, bf16[3,3,3,16,384]{4,3,2,1,0:T(8,128)(2,1)}, u32[]{:S(2)}) copy-start(bf16[3,3,3,16,384]{4,3,2,1,0:T(8,128)(2,1)} %cin_ref.1) | copy-start | bytes 995332
  2.0 17.7 %copy-start.4 = (s32[16,1]{1,0:T(8,128)}, s32[16,1]{1,0:T(8,128)S(1)}, u32[]{:S(2)}) copy-start(s32[16,1]{1,0:T(8,128)S(1)} %copy.16.group_ref) | copy-start | bytes 196
  19.7 2.1 %copy-start = (bf16[4,768,768]{2,1,0:T(8,128)(2,1)}, bf16[4,768,768]{2,1,0:T(8,128)(2,1)S(1)}, u32[]{:S(2)}) copy-start(bf16[4,768,768]{2,1,0:T(8,128)(2,1)S(1)} %get-tuple-element.9.band_hbm) | copy-start | bytes 14155780
  21.8 1.4 %copy-start.1 = (bf16[2,768,768]{2,1,0:T(8,128)(2,1)}, bf16[2,768,768]{2,1,0:T(8,128)(2,1)S(1)}, u32[]{:S(2)}) copy-start(bf16[2,768,768]{2,1,0:T(8,128)(2,1)S(1)} %get-tuple-element.10.up_hbm) | copy-start | bytes 7077892
  23.3 0.8 %copy-start.2 = (bf16[2,5,4,48,128]{4,3,2,1,0:T(8,128)(2,1)}, bf16[2,5,4,48,128]{4,3,2,1,0:T(8,128)(2,1)S(1)}, u32[]{:S(2)}) copy-start(bf16[2,5,4,48,128]{4,3,2,1,0:T(8,128)(2,1)S(1)} %get-tuple-element.8.recv_ref) | copy-start | bytes 1474564

commit v2 on v1

--- a/solution.py
+++ b/solution.py
@@ -24,7 +24,23 @@
 
 
 def exchange_kernel(
-    groups, tiles, group_ref, lat_ref, cin_ref, cup_ref, recv_ref, band_ref, up_ref, out_ref, send_sem, recv_sem, fwd_send, fwd_recv
+    groups,
+    tiles,
+    group_ref,
+    lat_ref,
+    cin_ref,
+    cup_ref,
+    mid_hbm,
+    recv_ref,
+    band_ref,
+    up_ref,
+    mid_ref,
+    out_ref,
+    send_sem,
+    recv_sem,
+    fwd_send,
+    fwd_recv,
+    mid_sem,
 ):
     src, tm, tile = lax.axis_index("src"), lax.axis_index("tm"), lax.axis_index("tile")
     clips = 4
@@ -34,6 +50,18 @@
         return jnp.logical_and(tile + d >= 0, tile + d < tiles)
 
     partners = [(k, d) for d in (0, 1, -1, 2, -2) for k in range(groups) if (k, d) != (0, 0)]
+
+    n = cin_ref.shape[-1]
+    mids = [
+        pltpu.make_async_copy(
+            mid_hbm.at[a, b, c], mid_ref.at[a, pl.ds(b * n, n), pl.ds(c * n, n)], mid_sem.at[a, b, c]
+        )
+        for a in (2, 1, 0)
+        for b in range(3)
+        for c in range(3)
+    ]
+    for mid in mids:
+        mid.start()
 
     barrier = pltpu.get_barrier_semaphore()
     for k, d in partners:
@@ -50,10 +78,10 @@
             rank_of = []
             total = jnp.zeros((lat_ref.shape[0], 128), F32)
             for i in range(clips):
-                target = group_ref[src * clips + i, 0]
+                target = group_ref[src * clips + i]
                 rank = jnp.int32(0)
                 for e in range(i):
-                    rank = rank + jnp.where(group_ref[src * clips + e, 0] == target, 1, 0)
+                    rank = rank + jnp.where(group_ref[src * clips + e] == target, 1, 0)
                 mine = jnp.where(jnp.logical_and(target == g, rank == k), 1.0, 0.0)
                 block = lat_ref[:, 128 * (i // 2) : 128 * (i // 2) + 128].astype(F32)
                 if i % 2 != k:
@@ -96,7 +124,6 @@
         recv_ref[1] = jnp.zeros(recv_ref.shape[1:], BF)
 
     zero = jnp.zeros((16, cin_ref.shape[-1]), BF)
-    n = cin_ref.shape[-1]
     for f in range(FR):
         for c in range(3):
             for row in range(4):
@@ -108,24 +135,16 @@
                         at = ((c * 4 + row) * FR + t) * 16
                         band_ref[f, at : at + 16, q * n : (q + 1) * n] = value
 
-    depth, width = cup_ref.shape[-2:]
-    step = 96
-    def fold(s, _):
-        at = pl.multiple_of(s * step, step)
+    def fold():
+        width, depth = cup_ref.shape[-2:]
         for p in range(2):
             for i in range(2):
                 rows = ((0,), (1, 2)) if p == 0 else ((0, 1), (2,))
-                per_c = []
-                for c in range(3):
-                    terms = [cup_ref[b, c, pl.ds(at, step), :].astype(F32) for b in rows[i]]
-                    per_c.append(functools.reduce(jnp.add, terms))
-                k0, k1, k2 = per_c
-                up_ref[p, pl.ds(i * depth + at, step), :] = jnp.concatenate(
-                    [k1 + k2, k0 + k1, k0, k2], axis=-1
-                ).astype(BF)
-        return 0
-
-    lax.fori_loop(0, depth // step, fold, 0)
+                k0, k1, k2 = [
+                    functools.reduce(jnp.add, [cup_ref[b, c].astype(F32) for b in rows[i]]) for c in range(3)
+                ]
+                for at, value in enumerate((k1 + k2, k0 + k1, k0, k2)):
+                    up_ref[p, at * width : (at + 1) * width, i * depth : (i + 1) * depth] = value.astype(BF)
 
     def forward(d):
         return pltpu.make_async_remote_copy(
@@ -158,6 +177,8 @@
         def _(d=d):
             forward(d).start()
 
+    fold()
+
     for k, d in partners:
         @pl.when(ok(d))
         def _(k=k, d=d):
@@ -171,6 +192,9 @@
         @pl.when(tm == 1)
         def _(d=d):
             forward(d).wait_recv()
+
+    for mid in mids:
+        mid.wait()
 
 
 def decode_kernel(
@@ -180,14 +204,11 @@
     frames_ref,
     recv_ref,
     gain_ref,
-    band_hbm,
-    mid_hbm,
-    up_hbm,
-    out_hbm,
-    count_ref,
     band_ref,
     mid_ref,
     up_ref,
+    out_hbm,
+    count_ref,
     z_ref,
     act_ref,
     hid_ref,
@@ -197,9 +218,6 @@
     o_ref,
     zero_ref,
     used_ref,
-    band_sem,
-    mid_sem,
-    up_sem,
     zero_sem,
     o_sem,
 ):
@@ -209,31 +227,12 @@
     Wd = z_ref.shape[1]
     top, bottom = tile == 0, tile == tiles - 1
 
-    bands = [pltpu.make_async_copy(band_hbm.at[f], band_ref.at[f], band_sem.at[f]) for f in range(FR)]
-    for band in bands:
-        band.start()
-    mids = []
-    for a in (2, 1, 0):
-        for b in range(3):
-            for c in range(3):
-                mids.append(
-                    pltpu.make_async_copy(
-                        mid_hbm.at[a, b, c],
-                        mid_ref.at[a, pl.ds(b * C, C), pl.ds(c * C, C)],
-                        mid_sem.at[a, b, c],
-                    )
-                )
-    for mid in mids:
-        mid.start()
-    ups = pltpu.make_async_copy(up_hbm, up_ref, up_sem)
-    ups.start()
-
     for s in range(slots):
         count_ref[s] = 0
     for s in range(groups):
         seen = jnp.int32(0)
         for i in range(clips):
-            hit = group_ref[s * clips + i, 0] == src
+            hit = group_ref[s * clips + i] == src
 
             @pl.when(hit)
             def _(s=s, i=i, seen=seen):
@@ -257,12 +256,10 @@
 
     each_dead(lambda c: c.start())
     used_ref[0] = 0
-    for band in bands:
-        band.wait()
 
     lane = lax.broadcasted_iota(jnp.int32, (Wd, 128), 1)
     spot = lax.broadcasted_iota(jnp.int32, (Wd, 1), 0)
-    gain = gain_ref[...]
+    gain = gain_ref[...].reshape(1, C)
 
     def first(s, _):
         n = count_ref[s]
@@ -299,8 +296,8 @@
                         hb = h[:, q * C : (q + 1) * C].astype(BF)
                         hf = hb.astype(F32)
                         ms = jnp.sum(hf * hf, axis=-1, keepdims=True) * (1.0 / C)
-                        x = hf * lax.rsqrt(ms + 1e-06) * gain
-                        act = x / (1.0 + jnp.exp(-x))
+                        x = hf * (0.5 * lax.rsqrt(ms + 1e-06)) * gain
+                        act = x + x * jnp.tanh(x)
                         for j in range(3):
                             part = act[j * Wd : (j + 1) * Wd]
                             if j == 0:
@@ -314,10 +311,6 @@
         return 0
 
     lax.fori_loop(0, slots, first, 0)
-    for mid in mids:
-        mid.wait()
-    ups.wait()
-
     spot4 = lax.broadcasted_iota(jnp.int32, (4, Wd, 1), 1)
     spot2 = lax.broadcasted_iota(jnp.int32, (2, Wd, 1), 1)
     left = lax.broadcasted_iota(jnp.int32, (2, Wd, C), 2) < C // 2
@@ -328,15 +321,16 @@
 
         @pl.when(f < count_ref[s])
         def _():
-            acc_ref[...] = jnp.zeros(acc_ref.shape, F32)
-
-            def tap(a, _):
-                x = act_ref[s, f - 2 + a]
-                lhs = jnp.concatenate([x[b : b + 4].reshape(4 * Wd, C) for b in range(3)], axis=1)
-                acc_ref[...] += jnp.dot(lhs, mid_ref[a], preferred_element_type=F32)
-                return 0
-
-            lax.fori_loop(jnp.maximum(2 - f, 0), 3, tap, 0)
+            for taps in range(1, 4):
+                @pl.when(taps == jnp.minimum(f + 1, 3))
+                def _():
+                    lhs = jnp.concatenate(
+                        [act_ref[s, f + a - 2, b : b + 4].reshape(4 * Wd, C) for a in range(3 - taps, 3) for b in range(3)],
+                        axis=1,
+                    )
+                    rhs = mid_ref[3 - taps :].reshape(taps * 3 * C, 3 * C)
+                    acc_ref[...] = jnp.dot(lhs, rhs, preferred_element_type=F32)
+
             total = acc_ref[:, C : 2 * C].reshape(4, Wd, C) + hid_ref[s, f].astype(F32)
             total = total + shift_down(acc_ref[:, :C].reshape(4, Wd, C), spot4 == 0)
             total = total + shift_up(acc_ref[:, 2 * C :].reshape(4, Wd, C), spot4 == Wd - 1)
@@ -352,7 +346,7 @@
                 lhs = jnp.concatenate(
                     [res_ref[p : p + 2].reshape(2 * Wd, C), res_ref[p + 1 : p + 3].reshape(2 * Wd, C)], axis=1
                 )
-                y = jnp.dot(lhs, up_ref[p], preferred_element_type=F32)
+                y = lax.dot_general(lhs, up_ref[p], (((1,), (1,)), ((), ())), preferred_element_type=F32)
                 still = y[:, :C].reshape(2, Wd, C)
                 moved = y[:, C:].reshape(2, Wd, C)
                 y = still + jnp.where(left, shift_down(moved, spot2 == 0), shift_up(moved, spot2 == Wd - 1))
@@ -394,41 +388,41 @@
     out_c = conv_up.shape[-1]
     slots = groups * CAP
     lat = latents.reshape(clips, slab, rows, width, lc).transpose(3, 0, 2, 1, 4).reshape(width, -1)
+    group = decoder_group.reshape(-1)
     vmem = pl.BlockSpec(memory_space=pltpu.VMEM)
     smem = pl.BlockSpec(memory_space=pltpu.SMEM)
-    hbm = pl.BlockSpec(memory_space=pl.ANY)
+    hbm = pl.BlockSpec(memory_space=pltpu.HBM)
     taps = 2 * REACH + 1
-    recv, band, up = pl.pallas_call(
+    recv, band, up, mid = pl.pallas_call(
         functools.partial(exchange_kernel, groups, tiles),
         out_shape=(
             jax.ShapeDtypeStruct((2, taps, groups, width, 128), BF),
             jax.ShapeDtypeStruct((FR, 3 * 4 * FR * lc, 2 * C), BF),
-            jax.ShapeDtypeStruct((2, 2 * C, 4 * out_c), BF),
+            jax.ShapeDtypeStruct((2, 4 * out_c, 2 * C), BF),
+            jax.ShapeDtypeStruct((3, 3 * C, 3 * C), BF),
         ),
-        in_specs=[smem, vmem, vmem, vmem],
-        out_specs=(vmem, vmem, vmem),
+        in_specs=[smem, vmem, vmem, vmem, hbm],
+        out_specs=(vmem, vmem, vmem, vmem),
         scratch_shapes=[
             pltpu.VMEM((groups, width, 128), BF),
             pltpu.SemaphoreType.DMA((taps, groups)),
             pltpu.SemaphoreType.DMA((taps, groups)),
             pltpu.SemaphoreType.DMA((taps,)),
             pltpu.SemaphoreType.DMA((taps,)),
+            pltpu.SemaphoreType.DMA((3, 3, 3)),
         ],
         compiler_params=pltpu.CompilerParams(
-            collective_id=0, has_side_effects=True, vmem_limit_bytes=32 * 1024 * 1024
+            collective_id=0, has_side_effects=True, vmem_limit_bytes=33 * 1024 * 1024
         ),
-    )(decoder_group, lat, conv_in, conv_up)
+    )(group, lat, conv_in, conv_up.transpose(0, 1, 3, 2), conv_mid)
 
     return pl.pallas_call(
         functools.partial(decode_kernel, groups, tiles),
         out_shape=jax.ShapeDtypeStruct((slots, slab, 2 * rows, 2 * width * out_c), BF),
-        in_specs=[smem, smem, vmem, vmem, hbm, hbm, hbm],
+        in_specs=[smem, smem, vmem, vmem, vmem, vmem, vmem],
         out_specs=hbm,
         scratch_shapes=[
             pltpu.SMEM((slots,), jnp.int32),
-            pltpu.VMEM(band.shape, BF),
-            pltpu.VMEM((3, 3 * C, 3 * C), BF),
-            pltpu.VMEM(up.shape, BF),
             pltpu.VMEM((3, width, 4 * FR * lc * 2), BF),
             pltpu.VMEM((slots, FR, 6, width, C), BF),
             pltpu.VMEM((slots, FR, 4, width, C), BF),
@@ -438,14 +432,11 @@
             pltpu.VMEM((2, 2 * rows, 2 * width * out_c), BF),
             pltpu.VMEM((2 * rows, 2 * width * out_c), BF),
             pltpu.SMEM((1,), jnp.int32),
-            pltpu.SemaphoreType.DMA((FR,)),
-            pltpu.SemaphoreType.DMA((3, 3, 3)),
-            pltpu.SemaphoreType.DMA,
             pltpu.SemaphoreType.DMA((slots, 2)),
             pltpu.SemaphoreType.DMA((2,)),
         ],
-        compiler_params=pltpu.CompilerParams(vmem_limit_bytes=56 * 1024 * 1024),
-    )(decoder_group, frames, recv, norm_gain.reshape(1, C), band, conv_mid, up)
+        compiler_params=pltpu.CompilerParams(vmem_limit_bytes=24 * 1024 * 1024),
+    )(group, frames, recv, norm_gain, band, mid, up)
 
 
 def solution(mesh):

time: 53.8 us -> 41.5 us (0.77)
  the two profiles are of different devices: /device:TPU:39 before, /device:TPU:4 now
where the time goes in v2:
time: 41.5 us; the launch traced here: 41.1 us
  Pallas kernels  37 us (89%)
  local copies, waits for them, and re-layouts  4.09 us (10%)
    pallas_call x1, Pallas kernels, per_device(): pl.pallas_call(functools.partial(decode_kernel, groups, tiles), out_shape...  22.1 us
    pallas_call x1, Pallas kernels, per_device(): pl.pallas_call(functools.partial(exchange_kernel, groups, tiles), out_sha...  14.9 us
    unnamed x10, local copies, waits for them, and re-layouts  2.95 us
    reshape x2, local copies, waits for them, and re-layouts, per_device(): latents.reshape(clips, slab, rows, width, lc).transpose(3, 0, 2, 1, 4)  1.02 us

profile of v2, /device:TPU:4, one launch (start us, length us, event | category | flops | bytes accessed | tf_op | source)
XLA Modules:
  0.0 41.1 jit_solution(9827722459913089996)
XLA Ops:
  0.0 0.9 %reshape.10 = bf16[4,2,2,48,16]{4,3,2,1,0:T(8,128)(2,1)S(1)} reshape(bf16[4,2,2,768]{3,2,1,0:T(2,128)(2,1)} %param.7) | data formatting | bytes 49152 | tf_op jit(solution)/shard_map/reshape | solution.py:390
  0.9 0.1 copy.9
  1.1 0.1 copy.10.lat_ref
  1.2 0.0 copy-start
  1.2 1.3 %copy-done = bf16[3,3,384,192]{2,3,1,0:T(8,128)(2,1)S(1)} copy-done((bf16[3,3,384,192]{2,3,1,0:T(8,128)(2,1)S(1)}, bf16[3,3,384,192]{2,3,1,0:T(8,128)(2,1)}, u32[]{:S(2)}) %copy-start) | copy-done | bytes 1327128
  2.5 0.0 copy-start.1
  2.5 1.0 %copy-done.1 = bf16[3,3,3,16,384]{4,3,2,1,0:T(8,128)(2,1)S(1)} copy-done((bf16[3,3,3,16,384]{4,3,2,1,0:T(8,128)(2,1)S(1)}, bf16[3,3,3,16,384]{4,3,2,1,0:T(8,128)(2,1)}, u32[]{:S(2)}) %copy-start.1) | copy-done | bytes 331800
  3.5 0.0 copy-start.2
  3.5 0.7 %copy-done.2 = s32[16,1]{0,1:T(1,128)S(1)} copy-done((s32[16,1]{0,1:T(1,128)S(1)}, s32[16,1]{0,1:T(1,128)}, u32[]{:S(2)}) %copy-start.2) | copy-done | bytes 88
  4.1 0.0 copy-start.3
  4.1 0.0 copy-start.4
  4.1 14.9 %shard_map.73 = (bf16[2,5,4,48,128]{4,3,2,1,0:T(8,128)(2,1)S(1)}, bf16[4,768,768]{2,1,0:T(8,128)(2,1)S(1)}, bf16[2,768,768]{2,1,0:T(8,128)(2,1)S(1)}, bf16[3,1152,1152]{2,1,0:T(8,128)(2,1)S(1)}) custom-call(s32[16]{0:T(128)S(1)} %bitcast.5, bf16[48,256]{1,0:T(8,128)(2,1)S(1)} %copy.10.lat_ref, bf16[3,3,3,16,384]{4,3,2,1,0:T(8,128)(2,1)S(1)} %copy-done.1, ...), custom_call_target="tpu_custom_call" | custom-call | tf_op jit(solution)/shard_map/pallas_call | solution.py:396
  19.0 0.0 copy-done.3
  19.0 0.0 copy-done.4
  19.1 22.1 %shard_map.74 = bf16[8,2,4,18432]{3,2,1,0:T(4,128)(2,1)} custom-call(s32[16]{0:T(128)S(1)} %bitcast.6, s32[16]{0:T(128)S(1)} %copy-done.4, bf16[2,5,4,48,128]{4,3,2,1,0:T(8,128)(2,1)S(1)} %get-tuple-element.9.recv_ref, f32[384]{0:T(512)S(1)} %copy-done.3, bf16[4,768,768]{2,1,0:T(8,128)(2,1)S(1)} %get-tuple-element.10.band_ref, ...), custom_call_target="tpu_custom_call" | custom-call | tf_op jit(solution)/shard_map/pallas_call | solution.py:419
Async XLA Ops:
  1.2 1.3 %copy-start = (bf16[3,3,384,192]{2,3,1,0:T(8,128)(2,1)S(1)}, bf16[3,3,384,192]{2,3,1,0:T(8,128)(2,1)}, u32[]{:S(2)}) copy-start(bf16[3,3,384,192]{2,3,1,0:T(8,128)(2,1)} %param.13) | copy-start | bytes 3981316
  2.5 1.0 %copy-start.1 = (bf16[3,3,3,16,384]{4,3,2,1,0:T(8,128)(2,1)S(1)}, bf16[3,3,3,16,384]{4,3,2,1,0:T(8,128)(2,1)}, u32[]{:S(2)}) copy-start(bf16[3,3,3,16,384]{4,3,2,1,0:T(8,128)(2,1)} %cin_ref.1) | copy-start | bytes 995332
  3.5 0.7 %copy-start.2 = (s32[16,1]{0,1:T(1,128)S(1)}, s32[16,1]{0,1:T(1,128)}, u32[]{:S(2)}) copy-start(s32[16,1]{0,1:T(1,128)} %param.8) | copy-start | bytes 196
  4.1 14.9 %copy-start.3 = (f32[384]{0:T(512)S(1)}, f32[384]{0:T(512)}, u32[]{:S(2)}) copy-start(f32[384]{0:T(512)} %gain_ref.1) | copy-start | bytes 4612
  4.1 14.9 %copy-start.4 = (s32[16]{0:T(128)S(1)}, s32[16]{0:T(128)}, u32[]{:S(2)}) copy-start(s32[16]{0:T(128)} %frames_ref.1) | copy-start | bytes 196

commit v3 on v2

v3 whole, which is shorter than its diff:
```python
import functools

import jax
import jax.numpy as jnp
from jax import lax
from jax.experimental import pallas as pl
from jax.experimental.pallas import tpu as pltpu
from jax.sharding import PartitionSpec as P

CAP = 2
FR = 4
REACH = 2
MESH = pl.DeviceIdType.MESH
BF = jnp.bfloat16
F32 = jnp.float32


def shift_down(x, first):
    return jnp.where(first, 0.0, pltpu.roll(x, 1, x.ndim - 2))


def shift_up(x, last):
    return jnp.where(last, 0.0, pltpu.roll(x, x.shape[-2] - 1, x.ndim - 2))


def exchange_kernel(
    groups, tiles, group_ref, lat_ref, recv_ref, out_ref, send_sem, recv_sem, fwd_send, fwd_recv
):
    src, tm, tile = lax.axis_index("src"), lax.axis_index("tm"), lax.axis_index("tile")
    clips = 4

    def ok(d):
        return jnp.logical_and(tile + d >= 0, tile + d < tiles)

    partners = [(k, d) for d in (2, -2, 1, -1, 0) for k in (2, 1, 3, 0) if (k, d) != (0, 0)]

    barrier = pltpu.get_barrier_semaphore()
    for k, d in partners:
        @pl.when(ok(d))
        def _(k=k, d=d):
            pl.semaphore_signal(
                barrier, inc=1, device_id={"src": lax.rem(src + k, groups), "tile": tile + d}, device_id_type=MESH
            )
    pl.semaphore_signal(barrier, inc=1, device_id={"tm": 1 - tm}, device_id_type=MESH)

    blocks = []
    for i in range(clips):
        block = lat_ref[:, 128 * (i // 2) : 128 * (i // 2) + 128].astype(F32)
        blocks.append((block, pltpu.roll(block, 64, 1)))
    lane = lax.broadcasted_iota(jnp.int32, blocks[0][0].shape, 1)
    targets = [group_ref[src * clips + i] for i in range(clips)]
    ranks = []
    for i in range(clips):
        rank = jnp.int32(0)
        for e in range(i):
            rank = rank + jnp.where(targets[e] == targets[i], 1, 0)
        ranks.append(rank)
    for g in range(groups):
        parts = []
        for k in range(CAP):
            total = jnp.zeros(lane.shape, F32)
            for i in range(clips):
                mine = jnp.logical_and(targets[i] == g, ranks[i] == k)
                total = total + blocks[i][(i + k) % 2] * jnp.where(mine, 1.0, 0.0)
            parts.append(total)
        out_ref[g] = jnp.where(lane < 64, parts[0], parts[1]).astype(BF)

    for d in (-2, -1, 1, 2):
        @pl.when(jnp.logical_not(ok(d)))
        def _(d=d):
            recv_ref[tm, d + REACH] = jnp.zeros(recv_ref.shape[2:], BF)

    @pl.when(tm == 0)
    def _():
        recv_ref[1] = jnp.zeros(recv_ref.shape[1:], BF)

    recv_ref[tm, REACH, src] = out_ref[src]

    nd = jnp.int32(1)
    for d in (-2, -1, 1, 2):
        nd = nd + jnp.where(ok(d), 1, 0)
    pl.semaphore_wait(barrier, groups * nd)

    def copy(k, d):
        g = lax.rem(src + k, groups)
        return pltpu.make_async_remote_copy(
            src_ref=out_ref.at[g],
            dst_ref=recv_ref.at[tm, REACH - d, src],
            send_sem=send_sem.at[d + REACH, k],
            recv_sem=recv_sem.at[REACH - d, src],
            device_id={"src": g, "tile": tile + d},
            device_id_type=MESH,
        )

    for k, d in partners:
        @pl.when(ok(d))
        def _(k=k, d=d):
            copy(k, d).start()

    def forward(d):
        return pltpu.make_async_remote_copy(
            src_ref=recv_ref.at[0, d + REACH],
            dst_ref=recv_ref.at[0, d + REACH],
            send_sem=fwd_send.at[d + REACH],
            recv_sem=fwd_recv.at[d + REACH],
            device_id={"tm": 1 - tm},
            device_id_type=MESH,
        )

    for d in (0, 1, -1, 2, -2):
        for k in range(groups):
            if (k, d) == (0, 0):
                continue
            s = lax.rem(src + k, groups)

            @pl.when(ok(d))
            def _(d=d, s=s):
                pltpu.make_async_remote_copy(
                    src_ref=out_ref.at[0],
                    dst_ref=recv_ref.at[tm, d + REACH, s],
                    send_sem=send_sem.at[d + REACH, 0],
                    recv_sem=recv_sem.at[d + REACH, s],
                    device_id={"tm": 1 - tm},
                    device_id_type=MESH,
                ).wait_recv()

        @pl.when(tm == 0)
        def _(d=d):
            forward(d).start()

    for k, d in partners:
        @pl.when(ok(d))
        def _(k=k, d=d):
            copy(k, d).wait_send()

    for d in (0, 1, -1, 2, -2):
        @pl.when(tm == 0)
        def _(d=d):
            forward(d).wait_send()

        @pl.when(tm == 1)
        def _(d=d):
            forward(d).wait_recv()


def decode_kernel(
    groups,
    tiles,
    group_ref,
    frames_ref,
    recv_ref,
    gain_ref,
    cin_ref,
    mid_ref,
    cup_ref,
    out_hbm,
    count_ref,
    up_ref,
    turn_ref,
    z_ref,
    act_ref,
    hid_ref,
    acc_ref,
    res_ref,
    y_ref,
    o_ref,
    zero_ref,
    used_ref,
    zero_sem,
    o_sem,
):
    src, tm, tile = lax.axis_index("src"), lax.axis_index("tm"), lax.axis_index("tile")
    clips, slots = 4, groups * CAP
    C = gain_ref.shape[-1]
    Wd = z_ref.shape[1]
    top, bottom = tile == 0, tile == tiles - 1

    for s in range(slots):
        count_ref[s] = 0
    for s in range(groups):
        seen = jnp.int32(0)
        for i in range(clips):
            hit = group_ref[s * clips + i] == src

            @pl.when(hit)
            def _(s=s, i=i, seen=seen):
                count_ref[s * CAP + jnp.minimum(seen, CAP - 1)] = frames_ref[s * clips + i]

            seen = seen + jnp.where(hit, 1, 0)

    zero_ref[...] = jnp.zeros(zero_ref.shape, BF)

    def clear(s, o):
        return pltpu.make_async_copy(zero_ref, out_hbm.at[s, o], zero_sem.at[s, o])

    def each_dead(go):
        def body(s, _):
            for o in range(2):
                @pl.when(2 * tm + o >= count_ref[s])
                def _():
                    go(clear(s, o))
            return 0
        lax.fori_loop(0, slots, body, 0)

    each_dead(lambda c: c.start())

    width = cup_ref.shape[-2]
    for p in range(2):
        for i in range(2):
            rows = ((0,), (1, 2)) if p == 0 else ((0, 1), (2,))
            k0, k1, k2 = [
                functools.reduce(jnp.add, [cup_ref[b, c].astype(F32) for b in rows[i]]) for c in range(3)
            ]
            for at, value in enumerate((k1 + k2, k0 + k1, k0, k2)):
                turn_ref[at * width : (at + 1) * width, :] = value.astype(BF)
            up_ref[p, i * C : (i + 1) * C, :] = turn_ref[...].T

    lane = lax.broadcasted_iota(jnp.int32, (Wd, 128), 1)
    spot = lax.broadcasted_iota(jnp.int32, (Wd, 1), 0)
    gain = gain_ref[...].reshape(1, C)
    nothing = jnp.zeros((16, C), BF)

    def band(f):
        rows = []
        for c in range(3):
            for row in range(4):
                for t in range(FR):
                    a = t - f + 2
                    rows.append(
                        jnp.concatenate(
                            [
                                cin_ref[a, row - q, c] if 0 <= a <= 2 and 0 <= row - q <= 2 else nothing
                                for q in range(2)
                            ],
                            axis=1,
                        )
                    )
        return jnp.concatenate(rows, axis=0)

    def hidden(s, frames):
        lhs = jnp.concatenate(
            [
                jnp.concatenate([z_ref[c, :, 128 * j : 128 * j + 256] for c in range(3)], axis=1)
                for j in range(3)
            ],
            axis=0,
        )
        for f in frames:
            h = jnp.dot(lhs, band(f), preferred_element_type=F32)
            for q in range(2):
                hb = h[:, q * C : (q + 1) * C].astype(BF)
                hf = hb.astype(F32)
                ms = jnp.sum(hf * hf, axis=-1, keepdims=True) * (1.0 / C)
                x = hf * (0.5 * lax.rsqrt(ms + 1e-06)) * gain
                act = x + x * jnp.tanh(x)
                for j in range(3):
                    part = act[j * Wd : (j + 1) * Wd]
                    if j == 0:
                        part = jnp.where(top, 0.0, part)
                    if j == 2:
                        part = jnp.where(bottom, 0.0, part)
                    r = 2 * j + q
                    act_ref[s, f, r] = part.astype(BF)
                    if 1 <= r <= 4:
                        hid_ref[s, f, r - 1] = hb[j * Wd : (j + 1) * Wd]

    def first(s, _):
        n = count_ref[s]
        need = jnp.where(tm == 0, jnp.minimum(n, 2), jnp.where(n >= 3, n, 0))

        @pl.when(need > 0)
        def _():
            sender, k = s // CAP, lax.rem(s, CAP)
            for m in range(4):
                upper = [recv_ref[h, m, sender].astype(F32) for h in range(2)]
                lower = [recv_ref[h, m + 1, sender].astype(F32) for h in range(2)]
                z0 = pltpu.roll(upper[0], 96 - 64 * k, 1)
                z1 = pltpu.roll(upper[1], lax.rem(128 - 64 * k, 128), 1)
                z2 = pltpu.roll(lower[0], 64 - 64 * k, 1)
                z3 = pltpu.roll(lower[1], 96 - 64 * k, 1)
                z = jnp.where(lane < 32, z0, jnp.where(lane < 64, z1, jnp.where(lane < 96, z2, z3)))
                at = slice(128 * m, 128 * m + 128)
                z_ref[0, :, at] = shift_down(z, spot == 0).astype(BF)
                z_ref[1, :, at] = z.astype(BF)
                z_ref[2, :, at] = shift_up(z, spot == Wd - 1).astype(BF)

        for frames, when in (
            ((0,), need == 1),
            ((0, 1), need >= 2),
            ((2,), need == 3),
            ((2, 3), need == 4),
        ):
            @pl.when(when)
            def _(frames=frames):
                hidden(s, frames)
        return 0

    lax.fori_loop(0, slots, first, 0)

    spot4 = lax.broadcasted_iota(jnp.int32, (4, Wd, 1), 1)
    spot2 = lax.broadcasted_iota(jnp.int32, (2, Wd, 1), 1)
    left = lax.broadcasted_iota(jnp.int32, (2, Wd, C), 2) < C // 2
    for e in range(5):
        used_ref[e] = 0

    def drain(buf):
        for e in range(2):
            @pl.when(used_ref[1 + 2 * buf + e] == 1)
            def _(e=e):
                pltpu.make_async_copy(o_ref.at[buf, e], out_hbm.at[0, 0], o_sem.at[buf, e]).wait()
                used_ref[1 + 2 * buf + e] = 0

    def finish(s, units):
        count = len(units)
        used = used_ref[0]
        buf = lax.rem(used, 2)
        for e, (o, taps) in enumerate(units):
            f = 2 * tm + o
            lhs = jnp.concatenate(
                [act_ref[s, f + a - 2, b : b + 4].reshape(4 * Wd, C) for a in range(3 - taps, 3) for b in range(3)],
                axis=1,
            )
            rhs = jnp.concatenate(
                [
                    jnp.concatenate([mid_ref[a, b, c] for c in range(3)], axis=1)
                    for a in range(3 - taps, 3)
                    for b in range(3)
                ],
                axis=0,
            )
            acc_ref[e] = jnp.dot(lhs, rhs, preferred_element_type=F32)

        drain(buf)

        for e, (o, taps) in enumerate(units):
            f = 2 * tm + o
            total = acc_ref[e, :, C : 2 * C].reshape(4, Wd, C) + hid_ref[s, f].astype(F32)
            total = total + shift_down(acc_ref[e, :, :C].reshape(4, Wd, C), spot4 == 0)
            total = total + shift_up(acc_ref[e, :, 2 * C :].reshape(4, Wd, C), spot4 == Wd - 1)
            for r in range(4):
                part = total[r]
                if r == 0:
                    part = jnp.where(top, 0.0, part)
                if r == 3:
                    part = jnp.where(bottom, 0.0, part)
                res_ref[e, r] = part.astype(BF)

        for p in range(2):
            lhs = jnp.concatenate(
                [
                    jnp.concatenate(
                        [res_ref[e, p : p + 2].reshape(2 * Wd, C), res_ref[e, p + 1 : p + 3].reshape(2 * Wd, C)],
                        axis=1,
                    )
                    for e in range(count)
                ],
                axis=0,
            )
            both = jnp.dot(lhs, up_ref[p], preferred_element_type=F32)
            for e in range(count):
                y = both[e * 2 * Wd : (e + 1) * 2 * Wd]
                still = y[:, :C].reshape(2, Wd, C)
                moved = y[:, C:].reshape(2, Wd, C)
                y = still + jnp.where(left, shift_down(moved, spot2 == 0), shift_up(moved, spot2 == Wd - 1))
                for h in range(2):
                    for v in range(C // 128):
                        y_ref[e, v, pl.ds((2 * h + p) * Wd, Wd), :] = y[h, :, v * 128 : v * 128 + 128]

        for e, (o, taps) in enumerate(units):
            for w in range(Wd):
                for v in range(C // 128):
                    at = w * C + v * 128
                    o_ref[buf, e, :, at : at + 128] = y_ref[e, v, pl.ds(w, 4, stride=Wd), :].astype(BF)
            pltpu.make_async_copy(o_ref.at[buf, e], out_hbm.at[s, o], o_sem.at[buf, e]).start()
            used_ref[1 + 2 * buf + e] = 1
        used_ref[0] = used + 1

    def second(s, _):
        n = count_ref[s]
        for units, when in (
            (((0, 1),), jnp.logical_and(tm == 0, n == 1)),
            (((0, 1), (1, 2)), jnp.logical_and(tm == 0, n >= 2)),
            (((0, 3),), jnp.logical_and(tm == 1, n == 3)),
            (((0, 3), (1, 3)), jnp.logical_and(tm == 1, n >= 4)),
        ):
            @pl.when(when)
            def _(units=units):
                finish(s, units)
        return 0

    lax.fori_loop(0, slots, second, 0)
    drain(0)
    drain(1)
    each_dead(lambda c: c.wait())


def per_device(latents, decoder_group, frames, conv_in, norm_gain, conv_mid, conv_up):
    groups, tiles = lax.axis_size("src"), lax.axis_size("tile")
    clips, slab, rows, packed = latents.shape
    lc, C = conv_in.shape[3:]
    width = packed // lc
    out_c = conv_up.shape[-1]
    slots = groups * CAP
    lat = latents.reshape(clips, slab, rows, width, lc).transpose(3, 0, 2, 1, 4).reshape(width, -1)
    group = decoder_group.reshape(-1)
    vmem = pl.BlockSpec(memory_space=pltpu.VMEM)
    smem = pl.BlockSpec(memory_space=pltpu.SMEM)
    hbm = pl.BlockSpec(memory_space=pltpu.HBM)
    taps = 2 * REACH + 1
    recv = pl.pallas_call(
        functools.partial(exchange_kernel, groups, tiles),
        out_shape=jax.ShapeDtypeStruct((2, taps, groups, width, 128), BF),
        in_specs=[smem, vmem],
        out_specs=vmem,
        scratch_shapes=[
            pltpu.VMEM((groups, width, 128), BF),
            pltpu.SemaphoreType.DMA((taps, groups)),
            pltpu.SemaphoreType.DMA((taps, groups)),
            pltpu.SemaphoreType.DMA((taps,)),
            pltpu.SemaphoreType.DMA((taps,)),
        ],
        compiler_params=pltpu.CompilerParams(
            collective_id=0, has_side_effects=True, vmem_limit_bytes=8 * 1024 * 1024
        ),
        cost_estimate=pl.CostEstimate(flops=40_000_000_000, bytes_accessed=40_000_000, transcendentals=0),
    )(group, lat)

    return pl.pallas_call(
        functools.partial(decode_kernel, groups, tiles),
        out_shape=jax.ShapeDtypeStruct((slots, slab, 2 * rows, 2 * width * out_c), BF),
        in_specs=[smem, smem, vmem, vmem, vmem, vmem, vmem],
        out_specs=hbm,
        scratch_shapes=[
            pltpu.SMEM((slots,), jnp.int32),
            pltpu.VMEM((2, 2 * C, 4 * out_c), BF),
            pltpu.VMEM((4 * out_c, C), BF),
            pltpu.VMEM((3, width, 4 * FR * lc * 2), BF),
            pltpu.VMEM((slots, FR, 6, width, C), BF),
            pltpu.VMEM((slots, FR, 4, width, C), BF),
            pltpu.VMEM((2, 4 * width, 3 * C), F32),
            pltpu.VMEM((2, 4, width, C), BF),
            pltpu.VMEM((2, C // 128, 4 * width, 128), F32),
            pltpu.VMEM((2, 2, 2 * rows, 2 * width * out_c), BF),
            pltpu.VMEM((2 * rows, 2 * width * out_c), BF),
            pltpu.SMEM((5,), jnp.int32),
            pltpu.SemaphoreType.DMA((slots, 2)),
            pltpu.SemaphoreType.DMA((2, 2)),
        ],
        compiler_params=pltpu.CompilerParams(vmem_limit_bytes=32 * 1024 * 1024),
    )(group, frames, recv, norm_gain, conv_in, conv_mid, conv_up.transpose(0, 1, 3, 2))


def solution(mesh):
    placed = (P("src", "tm", "tile", None), P(), P(), P(), P(), P(), P())
    return jax.shard_map(
        per_device,
        mesh=mesh,
        in_specs=placed,
        out_specs=P("src", "tm", "tile", None),
        check_vma=False,
    )
```

time: 41.5 us -> 34.6 us (0.83)
  the two profiles are of different devices: /device:TPU:4 before, /device:TPU:100 now
where the time goes in v3:
time: 34.6 us; the launch traced here: 34.4 us
  Pallas kernels  32.3 us (93%)
  local copies, waits for them, and re-layouts  1.82 us (5%)
    pallas_call x1, Pallas kernels, per_device(): pl.pallas_call(functools.partial(decode_kernel, groups, tiles), out_shape...  19.9 us
    pallas_call x1, Pallas kernels, per_device(): pl.pallas_call(functools.partial(exchange_kernel, groups, tiles), out_sha...  12.4 us
    reshape x2, local copies, waits for them, and re-layouts, per_device(): latents.reshape(clips, slab, rows, width, lc).transpose(3, 0, 2, 1, 4)  1.02 us

profile of v3, /device:TPU:100, one launch (start us, length us, event | category | flops | bytes accessed | tf_op | source)
XLA Modules:
  0.0 34.4 jit_solution(14839467629666040911)
XLA Ops:
  0.0 0.9 %reshape.10 = bf16[4,2,2,48,16]{4,3,2,1,0:T(8,128)(2,1)S(1)} reshape(bf16[4,2,2,768]{3,2,1,0:T(2,128)(2,1)} %param.7) | data formatting | bytes 49152 | tf_op jit(solution)/shard_map/reshape | solution.py:404
  0.9 0.1 copy.9
  1.1 0.1 copy.10.lat_ref
  1.2 0.0 copy-start.4
  1.2 0.6 %copy-done.4 = s32[16,1]{0,1:T(1,128)S(1)} copy-done((s32[16,1]{0,1:T(1,128)S(1)}, s32[16,1]{0,1:T(1,128)}, u32[]{:S(2)}) %copy-start.4) | copy-done | bytes 88
  1.8 0.0 copy-start
  1.8 0.0 copy-start.1
  1.8 0.0 copy-start.2
  1.8 0.0 copy-start.3
  1.8 0.0 copy-start.5
  1.8 0.0 copy-start.6
  1.9 12.4 %shard_map.73.recv_ref = bf16[2,5,4,48,128]{4,3,2,1,0:T(8,128)(2,1)S(1)} custom-call(s32[16]{0:T(128)S(1)} %bitcast.5, bf16[48,256]{1,0:T(8,128)(2,1)S(1)} %copy.10.lat_ref), custom_call_target="tpu_custom_call" | custom-call | flops 40000000000 | bytes 40000000 | tf_op jit(solution)/shard_map/pallas_call | solution.py:410
  14.3 0.0 copy-done
  14.3 0.0 copy-done.1
  14.3 0.0 copy-done.2
  14.3 0.0 copy-done.3
  14.3 0.0 copy-done.5
  14.3 0.0 copy-done.6
  14.3 19.9 %shard_map.74 = bf16[8,2,4,18432]{3,2,1,0:T(4,128)(2,1)} custom-call(s32[16]{0:T(128)S(1)} %bitcast.6, s32[16]{0:T(128)S(1)} %copy-done.6, bf16[2,5,4,48,128]{4,3,2,1,0:T(8,128)(2,1)S(1)} %shard_map.73.recv_ref, f32[384]{0:T(512)S(1)} %copy-done.3, bf16[3,3,3,16,384]{4,3,2,1,0:T(8,128)(2,1)S(1)} %copy-done.2, bf16[3,3,3,384,384]{4,3,2,1,0:T(8,128)(2,1)S(1)} %copy-done, ...), custom_call_target="tpu_custom_call" | custom-call | tf_op jit(solution)/shard_map/pallas_call | solution.py:428
Async XLA Ops:
  1.2 0.7 %copy-start.4 = (s32[16,1]{0,1:T(1,128)S(1)}, s32[16,1]{0,1:T(1,128)}, u32[]{:S(2)}) copy-start(s32[16,1]{0,1:T(1,128)} %param.8) | copy-start | bytes 196
  1.8 12.5 %copy-start = (bf16[3,3,3,384,384]{4,3,2,1,0:T(8,128)(2,1)S(1)}, bf16[3,3,3,384,384]{4,3,2,1,0:T(8,128)(2,1)}, u32[]{:S(2)}) copy-start(bf16[3,3,3,384,384]{4,3,2,1,0:T(8,128)(2,1)} %mid_ref.1) | copy-start | bytes 23887876
  1.8 12.5 %copy-start.1 = (bf16[3,3,384,192]{2,3,1,0:T(8,128)(2,1)S(1)}, bf16[3,3,384,192]{2,3,1,0:T(8,128)(2,1)}, u32[]{:S(2)}) copy-start(bf16[3,3,384,192]{2,3,1,0:T(8,128)(2,1)} %param.13) | copy-start | bytes 3981316
  1.8 12.5 %copy-start.2 = (bf16[3,3,3,16,384]{4,3,2,1,0:T(8,128)(2,1)S(1)}, bf16[3,3,3,16,384]{4,3,2,1,0:T(8,128)(2,1)}, u32[]{:S(2)}) copy-start(bf16[3,3,3,16,384]{4,3,2,1,0:T(8,128)(2,1)} %cin_ref.1) | copy-start | bytes 995332
  1.8 12.5 %copy-start.3 = (f32[384]{0:T(512)S(1)}, f32[384]{0:T(512)}, u32[]{:S(2)}) copy-start(f32[384]{0:T(512)} %gain_ref.1) | copy-start | bytes 4612
  1.8 12.5 %copy-start.5 = (s32[16,1]{0,1:T(1,128)S(1)}, s32[16,1]{0,1:T(1,128)}, u32[]{:S(2)}) copy-start(s32[16,1]{0,1:T(1,128)} %param.8) | copy-start | bytes 196
  1.8 12.5 %copy-start.6 = (s32[16]{0:T(128)S(1)}, s32[16]{0:T(128)}, u32[]{:S(2)}) copy-start(s32[16]{0:T(128)} %frames_ref.1) | copy-start | bytes 196

commit v4 on v3

--- a/solution.py
+++ b/solution.py
@@ -24,13 +24,17 @@
 
 
 def exchange_kernel(
-    groups, tiles, group_ref, lat_ref, recv_ref, out_ref, send_sem, recv_sem, fwd_send, fwd_recv
+    groups, tiles, group_ref, lat_ref, mid_hbm, recv_ref, wide0_ref, wide1_ref, wide2_ref, wide3_ref, out_ref, mid_ref, send_sem, recv_sem, fwd_send, fwd_recv, mid_sem
 ):
     src, tm, tile = lax.axis_index("src"), lax.axis_index("tm"), lax.axis_index("tile")
     clips = 4
 
     def ok(d):
         return jnp.logical_and(tile + d >= 0, tile + d < tiles)
+
+    mids = [pltpu.make_async_copy(mid_hbm.at[a], mid_ref.at[a], mid_sem.at[a]) for a in range(3)]
+    for mid in mids:
+        mid.start()
 
     partners = [(k, d) for d in (2, -2, 1, -1, 0) for k in (2, 1, 3, 0) if (k, d) != (0, 0)]
 
@@ -97,6 +101,25 @@
         def _(k=k, d=d):
             copy(k, d).start()
 
+    depth, step = mid_ref.shape[3], 32
+    for a, mid in enumerate(mids):
+        mid.wait()
+
+        def turn(i, _, a=a):
+            at = pl.ds(pl.multiple_of(i * step, step), step)
+            for c in range(3):
+                g0, g1, g2 = [mid_ref[a, b, c, at, :] for b in range(3)]
+                even = 0.5 * (g0.astype(F32) + g2.astype(F32))
+                odd = 0.5 * g1.astype(F32)
+                lanes = slice(c * depth, (c + 1) * depth)
+                wide0_ref[a, at, lanes] = g0
+                wide1_ref[a, at, lanes] = (even + odd).astype(BF)
+                wide2_ref[a, at, lanes] = (even - odd).astype(BF)
+                wide3_ref[a, at, lanes] = g2
+            return 0
+
+        lax.fori_loop(0, depth // step, turn, 0)
+
     def forward(d):
         return pltpu.make_async_remote_copy(
             src_ref=recv_ref.at[0, d + REACH],
@@ -151,10 +174,14 @@
     recv_ref,
     gain_ref,
     cin_ref,
-    mid_ref,
+    wide0_ref,
+    wide1_ref,
+    wide2_ref,
+    wide3_ref,
     cup_ref,
     out_hbm,
     count_ref,
+    list_ref,
     up_ref,
     turn_ref,
     z_ref,
@@ -172,7 +199,7 @@
     src, tm, tile = lax.axis_index("src"), lax.axis_index("tm"), lax.axis_index("tile")
     clips, slots = 4, groups * CAP
     C = gain_ref.shape[-1]
-    Wd = z_ref.shape[1]
+    Wd = z_ref.shape[3]
     top, bottom = tile == 0, tile == tiles - 1
 
     for s in range(slots):
@@ -217,52 +244,59 @@
 
     lane = lax.broadcasted_iota(jnp.int32, (Wd, 128), 1)
     spot = lax.broadcasted_iota(jnp.int32, (Wd, 1), 0)
-    gain = gain_ref[...].reshape(1, C)
+    gain = 0.5 * gain_ref[...].reshape(1, C)
+    row = lax.broadcasted_iota(jnp.int32, (3 * Wd, 1), 0)
+    inside = jnp.logical_not(
+        jnp.logical_or(jnp.logical_and(top, row < Wd), jnp.logical_and(bottom, row >= 2 * Wd))
+    )
     nothing = jnp.zeros((16, C), BF)
 
     def band(f):
         rows = []
-        for c in range(3):
-            for row in range(4):
-                for t in range(FR):
-                    a = t - f + 2
-                    rows.append(
-                        jnp.concatenate(
-                            [
-                                cin_ref[a, row - q, c] if 0 <= a <= 2 and 0 <= row - q <= 2 else nothing
-                                for q in range(2)
-                            ],
-                            axis=1,
+        for h in range(f // 2 + 1):
+            for c in range(3):
+                for row in range(4):
+                    for t in (2 * h, 2 * h + 1):
+                        a = t - f + 2
+                        rows.append(
+                            jnp.concatenate(
+                                [
+                                    cin_ref[a, row - q, c] if 0 <= a <= 2 and 0 <= row - q <= 2 else nothing
+                                    for q in range(2)
+                                ],
+                                axis=1,
+                            )
                         )
-                    )
         return jnp.concatenate(rows, axis=0)
 
     def hidden(s, frames):
         lhs = jnp.concatenate(
             [
-                jnp.concatenate([z_ref[c, :, 128 * j : 128 * j + 256] for c in range(3)], axis=1)
+                jnp.concatenate(
+                    [z_ref[h, c, j] for h in range(frames[0] // 2 + 1) for c in range(3)], axis=1
+                )
                 for j in range(3)
             ],
             axis=0,
         )
-        for f in frames:
-            h = jnp.dot(lhs, band(f), preferred_element_type=F32)
+        all_h = jnp.dot(lhs, jnp.concatenate([band(f) for f in frames], axis=1), preferred_element_type=F32)
+        for e, f in enumerate(frames):
+            h = all_h[:, e * 2 * C : (e + 1) * 2 * C]
+            acts = {}
             for q in range(2):
-                hb = h[:, q * C : (q + 1) * C].astype(BF)
-                hf = hb.astype(F32)
+                hf = h[:, q * C : (q + 1) * C]
                 ms = jnp.sum(hf * hf, axis=-1, keepdims=True) * (1.0 / C)
-                x = hf * (0.5 * lax.rsqrt(ms + 1e-06)) * gain
+                x = hf * jnp.where(inside, lax.rsqrt(ms + 1e-06), 0.0) * gain
                 act = x + x * jnp.tanh(x)
                 for j in range(3):
-                    part = act[j * Wd : (j + 1) * Wd]
-                    if j == 0:
-                        part = jnp.where(top, 0.0, part)
-                    if j == 2:
-                        part = jnp.where(bottom, 0.0, part)
                     r = 2 * j + q
-                    act_ref[s, f, r] = part.astype(BF)
+                    acts[r] = act[j * Wd : (j + 1) * Wd]
                     if 1 <= r <= 4:
-                        hid_ref[s, f, r - 1] = hb[j * Wd : (j + 1) * Wd]
+                        hid_ref[s, f, (r - 1) % 2, (r - 1) // 2] = hf[j * Wd : (j + 1) * Wd].astype(BF)
+            for i in range(2):
+                d0, d1, d2, d3 = [acts[2 * i + e] for e in range(4)]
+                for e, value in enumerate((d0 - d2, d1 + d2, d2 - d1, d1 - d3)):
+                    act_ref[s, f, e, i] = value.astype(BF)
 
     def first(s, _):
         n = count_ref[s]
@@ -271,18 +305,22 @@
         @pl.when(need > 0)
         def _():
             sender, k = s // CAP, lax.rem(s, CAP)
-            for m in range(4):
-                upper = [recv_ref[h, m, sender].astype(F32) for h in range(2)]
-                lower = [recv_ref[h, m + 1, sender].astype(F32) for h in range(2)]
-                z0 = pltpu.roll(upper[0], 96 - 64 * k, 1)
-                z1 = pltpu.roll(upper[1], lax.rem(128 - 64 * k, 128), 1)
-                z2 = pltpu.roll(lower[0], 64 - 64 * k, 1)
-                z3 = pltpu.roll(lower[1], 96 - 64 * k, 1)
-                z = jnp.where(lane < 32, z0, jnp.where(lane < 64, z1, jnp.where(lane < 96, z2, z3)))
-                at = slice(128 * m, 128 * m + 128)
-                z_ref[0, :, at] = shift_down(z, spot == 0).astype(BF)
-                z_ref[1, :, at] = z.astype(BF)
-                z_ref[2, :, at] = shift_up(z, spot == Wd - 1).astype(BF)
+
+            def gather(h):
+                blocks = [recv_ref[h, d, sender].astype(F32) for d in range(2 * REACH + 1)]
+                outer = [pltpu.roll(b, 96 - 64 * k, 1) for b in blocks]
+                inner = [pltpu.roll(b, lax.rem(160 - 64 * k, 128), 1) for b in blocks[1:4]]
+                for j in range(3):
+                    z = jnp.where(lane < 32, outer[j], jnp.where(lane < 96, inner[j], outer[j + 2]))
+                    z_ref[h, 0, j] = shift_down(z, spot == 0).astype(BF)
+                    z_ref[h, 1, j] = z.astype(BF)
+                    z_ref[h, 2, j] = shift_up(z, spot == Wd - 1).astype(BF)
+
+            gather(0)
+
+            @pl.when(tm == 1)
+            def _():
+                gather(1)
 
         for frames, when in (
             ((0,), need == 1),
@@ -297,7 +335,6 @@
 
     lax.fori_loop(0, slots, first, 0)
 
-    spot4 = lax.broadcasted_iota(jnp.int32, (4, Wd, 1), 1)
     spot2 = lax.broadcasted_iota(jnp.int32, (2, Wd, 1), 1)
     left = lax.broadcasted_iota(jnp.int32, (2, Wd, C), 2) < C // 2
     for e in range(5):
@@ -310,40 +347,45 @@
                 pltpu.make_async_copy(o_ref.at[buf, e], out_hbm.at[0, 0], o_sem.at[buf, e]).wait()
                 used_ref[1 + 2 * buf + e] = 0
 
-    def finish(s, units):
+    def finish(units, taps):
         count = len(units)
+        M = 2 * Wd * count
         used = used_ref[0]
         buf = lax.rem(used, 2)
-        for e, (o, taps) in enumerate(units):
-            f = 2 * tm + o
+        for k in range(4):
             lhs = jnp.concatenate(
-                [act_ref[s, f + a - 2, b : b + 4].reshape(4 * Wd, C) for a in range(3 - taps, 3) for b in range(3)],
-                axis=1,
-            )
-            rhs = jnp.concatenate(
                 [
-                    jnp.concatenate([mid_ref[a, b, c] for c in range(3)], axis=1)
-                    for a in range(3 - taps, 3)
-                    for b in range(3)
+                    jnp.concatenate(
+                        [act_ref[s, 2 * tm + o + a - 2, k].reshape(2 * Wd, C) for a in range(3 - taps, 3)], axis=1
+                    )
+                    for s, o in units
                 ],
                 axis=0,
             )
-            acc_ref[e] = jnp.dot(lhs, rhs, preferred_element_type=F32)
+            rhs = (wide0_ref, wide1_ref, wide2_ref, wide3_ref)[k][3 - taps :].reshape(taps * C, 3 * C)
+            acc_ref[k, :M] = jnp.dot(lhs, rhs, preferred_element_type=F32)
 
         drain(buf)
 
-        for e, (o, taps) in enumerate(units):
+        for e, (s, o) in enumerate(units):
             f = 2 * tm + o
-            total = acc_ref[e, :, C : 2 * C].reshape(4, Wd, C) + hid_ref[s, f].astype(F32)
-            total = total + shift_down(acc_ref[e, :, :C].reshape(4, Wd, C), spot4 == 0)
-            total = total + shift_up(acc_ref[e, :, 2 * C :].reshape(4, Wd, C), spot4 == Wd - 1)
-            for r in range(4):
-                part = total[r]
-                if r == 0:
-                    part = jnp.where(top, 0.0, part)
-                if r == 3:
-                    part = jnp.where(bottom, 0.0, part)
-                res_ref[e, r] = part.astype(BF)
+            at = slice(e * 2 * Wd, (e + 1) * 2 * Wd)
+            for q in range(2):
+                def row(c):
+                    lanes = slice(c * C, (c + 1) * C)
+                    m = [acc_ref[k, at, lanes] for k in ((0, 1, 2), (1, 2, 3))[q]]
+                    return (m[0] + m[1] + m[2] if q == 0 else m[0] - m[1] - m[2]).reshape(2, Wd, C)
+
+                total = row(1) + hid_ref[s, f, q].astype(F32)
+                total = total + shift_down(row(0), spot2 == 0)
+                total = total + shift_up(row(2), spot2 == Wd - 1)
+                for i in range(2):
+                    part = total[i]
+                    if (i, q) == (0, 0):
+                        part = jnp.where(top, 0.0, part)
+                    if (i, q) == (1, 1):
+                        part = jnp.where(bottom, 0.0, part)
+                    res_ref[e, 2 * i + q] = part.astype(BF)
 
         for p in range(2):
             lhs = jnp.concatenate(
@@ -361,12 +403,20 @@
                 y = both[e * 2 * Wd : (e + 1) * 2 * Wd]
                 still = y[:, :C].reshape(2, Wd, C)
                 moved = y[:, C:].reshape(2, Wd, C)
-                y = still + jnp.where(left, shift_down(moved, spot2 == 0), shift_up(moved, spot2 == Wd - 1))
-                for h in range(2):
-                    for v in range(C // 128):
-                        y_ref[e, v, pl.ds((2 * h + p) * Wd, Wd), :] = y[h, :, v * 128 : v * 128 + 128]
-
-        for e, (o, taps) in enumerate(units):
+                for v in range(C // 128):
+                    at = slice(v * 128, v * 128 + 128)
+                    part = moved[..., at]
+                    if 2 * (v + 1) * 128 <= C:
+                        part = shift_down(part, spot2 == 0)
+                    elif 2 * v * 128 >= C:
+                        part = shift_up(part, spot2 == Wd - 1)
+                    else:
+                        part = jnp.where(left[..., at], shift_down(part, spot2 == 0), shift_up(part, spot2 == Wd - 1))
+                    part = part + still[..., at]
+                    for h in range(2):
+                        y_ref[e, v, pl.ds((2 * h + p) * Wd, Wd), :] = part[h]
+
+        for e, (s, o) in enumerate(units):
             for w in range(Wd):
                 for v in range(C // 128):
                     at = w * C + v * 128
@@ -375,20 +425,35 @@
             used_ref[1 + 2 * buf + e] = 1
         used_ref[0] = used + 1
 
-    def second(s, _):
-        n = count_ref[s]
-        for units, when in (
-            (((0, 1),), jnp.logical_and(tm == 0, n == 1)),
-            (((0, 1), (1, 2)), jnp.logical_and(tm == 0, n >= 2)),
-            (((0, 3),), jnp.logical_and(tm == 1, n == 3)),
-            (((0, 3), (1, 3)), jnp.logical_and(tm == 1, n >= 4)),
-        ):
-            @pl.when(when)
-            def _(units=units):
-                finish(s, units)
-        return 0
-
-    lax.fori_loop(0, slots, second, 0)
+    for kind in range(3):
+        list_ref[kind, 2 * slots] = 0
+    for s in range(slots):
+        for o in range(2):
+            kind = jnp.where(tm == 0, o, 2)
+
+            @pl.when(2 * tm + o < count_ref[s])
+            def _(s=s, o=o, kind=kind):
+                at = list_ref[kind, 2 * slots]
+                list_ref[kind, at] = 2 * s + o
+                list_ref[kind, 2 * slots] = at + 1
+
+    for kind in range(3):
+        total = list_ref[kind, 2 * slots]
+
+        def unit(i, kind=kind):
+            u = list_ref[kind, i]
+            return u // 2, lax.rem(u, 2)
+
+        def second(i, _, kind=kind, unit=unit):
+            finish((unit(2 * i), unit(2 * i + 1)), kind + 1)
+            return 0
+
+        lax.fori_loop(0, total // 2, second, 0)
+
+        @pl.when(lax.rem(total, 2) == 1)
+        def _(kind=kind, unit=unit, total=total):
+            finish((unit(total - 1),), kind + 1)
+
     drain(0)
     drain(1)
     each_dead(lambda c: c.wait())
@@ -407,37 +472,43 @@
     smem = pl.BlockSpec(memory_space=pltpu.SMEM)
     hbm = pl.BlockSpec(memory_space=pltpu.HBM)
     taps = 2 * REACH + 1
-    recv = pl.pallas_call(
+    recv, *wide = pl.pallas_call(
         functools.partial(exchange_kernel, groups, tiles),
-        out_shape=jax.ShapeDtypeStruct((2, taps, groups, width, 128), BF),
-        in_specs=[smem, vmem],
-        out_specs=vmem,
+        out_shape=(
+            jax.ShapeDtypeStruct((2, taps, groups, width, 128), BF),
+            *[jax.ShapeDtypeStruct((3, C, 3 * C), BF)] * 4,
+        ),
+        in_specs=[smem, vmem, hbm],
+        out_specs=(vmem,) * 5,
         scratch_shapes=[
             pltpu.VMEM((groups, width, 128), BF),
+            pltpu.VMEM(conv_mid.shape, BF),
             pltpu.SemaphoreType.DMA((taps, groups)),
             pltpu.SemaphoreType.DMA((taps, groups)),
             pltpu.SemaphoreType.DMA((taps,)),
             pltpu.SemaphoreType.DMA((taps,)),
+            pltpu.SemaphoreType.DMA((3,)),
         ],
         compiler_params=pltpu.CompilerParams(
-            collective_id=0, has_side_effects=True, vmem_limit_bytes=8 * 1024 * 1024
+            collective_id=0, has_side_effects=True, vmem_limit_bytes=38 * 1024 * 1024
         ),
         cost_estimate=pl.CostEstimate(flops=40_000_000_000, bytes_accessed=40_000_000, transcendentals=0),
-    )(group, lat)
+    )(group, lat, conv_mid)
 
     return pl.pallas_call(
         functools.partial(decode_kernel, groups, tiles),
         out_shape=jax.ShapeDtypeStruct((slots, slab, 2 * rows, 2 * width * out_c), BF),
-        in_specs=[smem, smem, vmem, vmem, vmem, vmem, vmem],
+        in_specs=[smem, smem] + [vmem] * 8,
         out_specs=hbm,
         scratch_shapes=[
             pltpu.SMEM((slots,), jnp.int32),
+            pltpu.SMEM((3, 2 * slots + 1), jnp.int32),
             pltpu.VMEM((2, 2 * C, 4 * out_c), BF),
             pltpu.VMEM((4 * out_c, C), BF),
-            pltpu.VMEM((3, width, 4 * FR * lc * 2), BF),
-            pltpu.VMEM((slots, FR, 6, width, C), BF),
-            pltpu.VMEM((slots, FR, 4, width, C), BF),
-            pltpu.VMEM((2, 4 * width, 3 * C), F32),
+            pltpu.VMEM((2, 3, 3, width, 128), BF),
+            pltpu.VMEM((slots, FR, 4, 2, width, C), BF),
+            pltpu.VMEM((slots, FR, 2, 2, width, C), BF),
+            pltpu.VMEM((4, 4 * width, 3 * C), F32),
             pltpu.VMEM((2, 4, width, C), BF),
             pltpu.VMEM((2, C // 128, 4 * width, 128), F32),
             pltpu.VMEM((2, 2, 2 * rows, 2 * width * out_c), BF),
@@ -447,7 +518,7 @@
             pltpu.SemaphoreType.DMA((2, 2)),
         ],
         compiler_params=pltpu.CompilerParams(vmem_limit_bytes=32 * 1024 * 1024),
-    )(group, frames, recv, norm_gain, conv_in, conv_mid, conv_up.transpose(0, 1, 3, 2))
+    )(group, frames, recv, norm_gain, conv_in, *wide, conv_up.transpose(0, 1, 3, 2))
 
 
 def solution(mesh):

time: 34.6 us -> 32.5 us (0.939)
  the two profiles are of different devices: /device:TPU:100 before, /device:TPU:68 now
where the time goes in v4:
time: 32.5 us; the launch traced here: 32.3 us
  Pallas kernels  30.3 us (93%)
  local copies, waits for them, and re-layouts  1.81 us (6%)
    pallas_call x1, Pallas kernels, per_device(): pl.pallas_call(functools.partial(decode_kernel, groups, tiles), out_shape...  17.8 us
    pallas_call x1, Pallas kernels, per_device(): pl.pallas_call(functools.partial(exchange_kernel, groups, tiles), out_sha...  12.5 us
    reshape x2, local copies, waits for them, and re-layouts, per_device(): latents.reshape(clips, slab, rows, width, lc).transpose(3, 0, 2, 1, 4)  1.02 us
    unnamed x10, local copies, waits for them, and re-layouts  0.67 us

profile of v4, /device:TPU:68, one launch (start us, length us, event | category | flops | bytes accessed | tf_op | source)
XLA Modules:
  0.0 32.3 jit_solution(18310025269621042520)
XLA Ops:
  0.0 0.9 %reshape.10 = bf16[4,2,2,48,16]{4,3,2,1,0:T(8,128)(2,1)S(1)} reshape(bf16[4,2,2,768]{3,2,1,0:T(2,128)(2,1)} %param.7) | data formatting | bytes 49152 | tf_op jit(solution)/shard_map/reshape | solution.py:469
  0.9 0.1 copy.9
  1.1 0.1 copy.10.lat_ref
  1.2 0.0 copy-start.3
  1.2 0.6 %copy-done.3 = s32[16,1]{0,1:T(1,128)S(1)} copy-done((s32[16,1]{0,1:T(1,128)S(1)}, s32[16,1]{0,1:T(1,128)}, u32[]{:S(2)}) %copy-start.3) | copy-done | bytes 88
  1.8 0.0 copy-start
  1.8 0.0 copy-start.1
  1.8 0.0 copy-start.2
  1.8 0.0 copy-start.4
  1.8 12.5 %shard_map.73 = (bf16[2,5,4,48,128]{4,3,2,1,0:T(8,128)(2,1)S(1)}, bf16[3,384,1152]{2,1,0:T(8,128)(2,1)S(1)}, bf16[3,384,1152]{2,1,0:T(8,128)(2,1)S(1)}, bf16[3,3...) custom-call(s32[16]{0:T(128)S(1)} %bitcast.5, bf16[48,256]{1,0:T(8,128)(2,1)S(1)} %copy.10.lat_ref, ...), custom_call_target="tpu_custom_call" | custom-call | flops 40000000000 | bytes 40000000 | tf_op jit(solution)/shard_map/pallas_call | solution.py:475
  14.4 0.0 copy-done
  14.4 0.0 copy-done.1
  14.4 0.0 copy-done.2
  14.4 0.0 copy-done.4
  14.4 17.8 %shard_map.74 = bf16[8,2,4,18432]{3,2,1,0:T(4,128)(2,1)} custom-call(s32[16]{0:T(128)S(1)} %bitcast.6, s32[16]{0:T(128)S(1)} %copy-done.4, bf16[2,5,4,48,128]{4,3,2,1,0:T(8,128)(2,1)S(1)} %get-tuple-element.10.recv_ref, f32[384]{0:T(512)S(1)} %copy-done.2, bf16[3,3,3,16,384]{4,3,2,1,0:T(8,128)(2,1)S(1)} %copy-done.1, ...), custom_call_target="tpu_custom_call" | custom-call | tf_op jit(solution)/shard_map/pallas_call | solution.py:498
Async XLA Ops:
  1.2 0.7 %copy-start.3 = (s32[16,1]{0,1:T(1,128)S(1)}, s32[16,1]{0,1:T(1,128)}, u32[]{:S(2)}) copy-start(s32[16,1]{0,1:T(1,128)} %param.8) | copy-start | bytes 196
  1.8 12.5 %copy-start = (bf16[3,3,384,192]{2,3,1,0:T(8,128)(2,1)S(1)}, bf16[3,3,384,192]{2,3,1,0:T(8,128)(2,1)}, u32[]{:S(2)}) copy-start(bf16[3,3,384,192]{2,3,1,0:T(8,128)(2,1)} %param.13) | copy-start | bytes 3981316
  1.8 12.6 %copy-start.1 = (bf16[3,3,3,16,384]{4,3,2,1,0:T(8,128)(2,1)S(1)}, bf16[3,3,3,16,384]{4,3,2,1,0:T(8,128)(2,1)}, u32[]{:S(2)}) copy-start(bf16[3,3,3,16,384]{4,3,2,1,0:T(8,128)(2,1)} %cin_ref.1) | copy-start | bytes 995332
  1.8 12.6 %copy-start.2 = (f32[384]{0:T(512)S(1)}, f32[384]{0:T(512)}, u32[]{:S(2)}) copy-start(f32[384]{0:T(512)} %gain_ref.1) | copy-start | bytes 4612
  1.8 12.6 %copy-start.4 = (s32[16]{0:T(128)S(1)}, s32[16]{0:T(128)}, u32[]{:S(2)}) copy-start(s32[16]{0:T(128)} %frames_ref.1) | copy-start | bytes 196
